TPU v7x, 128 devices: a whole 4x4x4 slice. The times are simulated.
128 devices in a mesh: size: 8 (over z, x_lo), gz: 16 (over x_hi, y, core).
Axes of the slice: x: 4 (x_hi: 2, x_lo: 2; x = x_hi * 2 + x_lo), y: 4, z: 4, core: 2. Of those that a mesh axis runs over, the one named last changes fastest.
Arguments:
- tissue: int32 [512, 128, 128], P('gz'), may hold values from 0 to 2
- vessel_pressure: float32 [512, 128, 128], P('gz', 'size'), may hold values from -12 to 12
- cond_table: float32 [3], replicated, may hold values from 0.4 to 1.2
- leak_table: float32 [3], replicated, may hold values from 0.2 to 2
- bind_table: float32 [8, 3], P('size'), may hold values from 0.05 to 1
- hindrance: float32 [8], P('size'), may hold values from 0.2 to 1
- diffusivity: float32 [8], P('size'), may hold values from 0.1 to 0.6
- free_conc: float32 [8, 512, 128, 128], P('size', 'gz'), may hold values from 0 to 2
- bound_conc: float32 [8, 512, 128, 128], P('size', 'gz'), may hold values from 0 to 1
Outputs:
- pressure: float32 [512, 128, 128], P('gz', 'size')
- free_out: float32 [8, 512, 128, 128], P('size', 'gz')
- bound_out: float32 [8, 512, 128, 128], P('size', 'gz')
Inputs may be any that keep to these rules, and one draw needn't show every extreme that they name: 0 marks a vessel cell, 1 necrotic tissue, 2 viable tissue.
All inputs are finite; a program needn't handle non-finite values.
Results may differ from a plain program's by a relative error of at most 0.0001.
Values sent between devices are 32-bit elements; how exact they have to be, the bound alone decides.
A program may use at most 128 MiB of HBM per device.

v0:
```python
import jax
import jax.numpy as jnp
from jax import lax
from jax.sharding import Mesh
from jax.sharding import PartitionSpec as P

ITERS = 2
TSTEPS = 2
SIZE_GZ = ("size_0", "size_1", "gz_0", "gz_1", "gz_2")
SIZE = ("size_0", "size_1")
GZ = ("gz_0", "gz_1", "gz_2")


time_step = 0.1


def extended(array, sides, width):
    edges = {}
    for axis, dim in sides:
        peers, length = (lax.axis_size(axis), array.shape[dim])
        up = [(i, (i + 1) % peers) for i in range(peers - 1)]
        last = lax.slice_in_dim(array, length - width, length, axis=dim)
        initial = lax.slice_in_dim(array, 0, width, axis=dim)
        edges[dim] = (
            lax.ppermute(last, axis, up),
            lax.ppermute(initial, axis, [(b, a) for a, b in up]),
        )
    done = []
    for _, dim in sides:
        low, high = edges[dim]
        around = [(width, width) if d in done else (0, 0) for d in range(array.ndim)]
        array = jnp.concatenate([jnp.pad(low, around), array, jnp.pad(high, around)], axis=dim)
        done.append(dim)
    return array


def by_axis(array, axes):
    for axis in axes:
        array = lax.psum(array, axis)
    return array


def from_everyone(array, axis):
    copies = jnp.broadcast_to(array, (lax.axis_size(axis), *array.shape))
    return lax.all_to_all(copies, axis, split_axis=0, concat_axis=0, tiled=True)


def in_order(blocks, dim):
    lengths = list(blocks.shape[1:])
    lengths[dim] *= blocks.shape[0]
    return jnp.moveaxis(blocks, 0, dim).reshape(lengths)


def gathered_copies(array, axis, dim):
    blocks = from_everyone(array, axis)
    return in_order(blocks, dim)


def extended_2(cells, sides, width):
    for axis, dim in sides:
        count = lax.axis_size(axis)
        ends = count - 1
        head = lax.slice_in_dim(cells, 0, width, axis=dim)
        tail = lax.slice_in_dim(cells, cells.shape[dim] - width, cells.shape[dim], axis=dim)
        cells = jnp.concatenate(
            [
                lax.ppermute(tail, axis, [(i, (i + 1) % count) for i in range(ends)]),
                cells,
                lax.ppermute(head, axis, [((i + 1) % count, i) for i in range(ends)]),
            ],
            axis=dim,
        )
    return cells


def lookup(table, labels):
    return jnp.where(labels == 0, table[0], jnp.where(labels == 1, table[1], table[2]))


def neighbours(padded):
    total = padded[2:, 1:-1, 1:-1] + padded[:-2, 1:-1, 1:-1]
    total = total + padded[1:-1, 2:, 1:-1] + padded[1:-1, :-2, 1:-1]
    total = total + padded[1:-1, 1:-1, 2:] + padded[1:-1, 1:-1, :-2]
    return total


def apply_operator(vector, conduct, leak):
    scaled = conduct * vector
    rimmed = extended(scaled, ((SIZE, 1), (GZ, 0)), 1)
    padded = jnp.pad(rimmed, ((0, 0), (0, 0), (1, 1)))
    return conduct * (6.0 * scaled - neighbours(padded)) + leak * vector


def paired_products(residual, precond, image):
    return (
        by_axis(jnp.sum(residual * precond), SIZE_GZ),
        by_axis(jnp.sum(precond * image), SIZE_GZ),
    )


def along_line(array, along_dim):
    return array[tuple((slice(None) if k == along_dim else slice(1, -1) for k in range(3)))]


def lower_part(array, along_dim):
    return array[tuple((slice(0, -1) if k == along_dim else slice(None) for k in range(3)))]


def upper_part(array, along_dim):
    return array[tuple((slice(1, None) if k == along_dim else slice(None) for k in range(3)))]


def transport_step(conc_pad, fields_pad, hinder, diffuse):
    divergence = None
    for along_dim in range(3):
        conc_line = along_line(conc_pad, along_dim)
        press_line = along_line(fields_pad[0], along_dim)
        cond_line = along_line(fields_pad[1], along_dim)
        conc_low = lower_part(conc_line, along_dim)
        conc_high = upper_part(conc_line, along_dim)
        velocity = (
            hinder
            * lower_part(cond_line, along_dim)
            * upper_part(cond_line, along_dim)
            * (lower_part(press_line, along_dim) - upper_part(press_line, along_dim))
        )
        flux = (
            jnp.maximum(velocity, 0.0) * conc_low
            + jnp.minimum(velocity, 0.0) * conc_high
            + diffuse * (conc_low - conc_high)
        )
        term = upper_part(flux, along_dim) - lower_part(flux, along_dim)
        divergence = term if divergence is None else divergence + term
    conc = conc_pad[1:-1, 1:-1, 1:-1]
    rate = fields_pad[2][1:-1, 1:-1, 1:-1]
    bind = rate * conc
    return (conc - time_step * (divergence + bind), bind)


def pad_plane(array):
    return jnp.pad(array, ((0, 0), (1, 1), (1, 1)))


def local(
    tissue,
    vessel_pressure,
    cond_table,
    leak_table,
    bind_table,
    hindrance,
    diffusivity,
    free_conc,
    bound_conc,
):
    block_x = vessel_pressure.shape[1]
    slab_z = vessel_pressure.shape[0]
    local_tissue = lax.dynamic_slice_in_dim(tissue, lax.axis_index(SIZE) * block_x, block_x, 1)
    conduct = lookup(cond_table, local_tissue)
    leak = lookup(leak_table, local_tissue)
    diag = 6.0 * conduct * conduct + leak
    source = leak * vessel_pressure
    solution = jnp.zeros_like(source)
    residual = source
    precond = residual / diag
    image = apply_operator(precond, conduct, leak)
    rho_now, product = paired_products(residual, precond, image)
    alpha = rho_now / product
    direction = precond
    along_image = image
    for iteration in range(ITERS):
        solution = solution + alpha * direction
        residual = residual - alpha * along_image
        if iteration + 1 < ITERS:
            precond = residual / diag
            image = apply_operator(precond, conduct, leak)
            rho_next, product = paired_products(residual, precond, image)
            ratio = rho_next / rho_now
            alpha = rho_next / (product - ratio * rho_next / alpha)
            direction = precond + ratio * direction
            along_image = image + ratio * along_image
            rho_now = rho_next
    conduct_slab = lookup(cond_table, tissue)
    rate_slab = lookup(bind_table[0], tissue)
    slab_pressure = gathered_copies(solution, SIZE, 1)
    stacked = jnp.stack([slab_pressure, conduct_slab, rate_slab])
    rimmed = extended_2(stacked, ((GZ, 1),), TSTEPS)
    fields_pad = jnp.pad(rimmed, ((0, 0), (0, 0), (1, 1), (1, 1)))
    hinder = hindrance[0]
    diffuse = diffusivity[0]
    conc = free_conc[0]
    bound = bound_conc[0]
    fields_one = fields_pad[:, TSTEPS - 1 : TSTEPS + 1 + slab_z]
    for sweep in range(TSTEPS):
        conc_pad = pad_plane(extended_2(conc, ((GZ, 0),), 1))
        conc, bind = transport_step(conc_pad, fields_one, hinder, diffuse)
        bound = bound + time_step * bind
    return (solution, conc[None], bound[None])


def solution(mesh):
    finer = Mesh(mesh.devices.reshape(4, 2, 2, 4, 2), ("size_0", "size_1", "gz_0", "gz_1", "gz_2"))
    return jax.shard_map(
        local,
        mesh=finer,
        in_specs=(
            P(GZ, None, None),
            P(GZ, SIZE, None),
            P(),
            P(),
            P(SIZE, None),
            P(SIZE),
            P(SIZE),
            P(SIZE, GZ, None, None),
            P(SIZE, GZ, None, None),
        ),
        out_specs=(P(GZ, SIZE, None), P(SIZE, GZ, None, None), P(SIZE, GZ, None, None)),
        check_vma=False,
    )
```

profile of v0, /device:TPU:6, one launch (start us, length us, event | category | flops | bytes accessed | tf_op | source)
XLA Modules:
  0.0 285.2 jit_solution(7565283562360594348)
XLA Ops:
  3.4 5.1 %fusion.39 = (f32[32,16,128]{2,1,0:T(8,128)S(1)}, pred[32,16,128]{2,1,0:T(8,128)(4,1)S(1)}, pred[32,16,128]{2,1,0:T(8,128)(4,1)S(1)}) fusion(f32[]{:T(128)} %bitcast.5, f32[]{:T(128)} %bitcast.4, f32[]{:T(128)} %bitcast.3, f32[32,16,128]{2,1,0:T(8,128)} %param.10, f32[]{:T(128)} %bitcast.2, f32[]{:T(128)} %bitcast.1, f32[]{:T(128)} %bitcast, ...), kind=kLoop, calls=%fused_computation.130 | loop fusion | flops 786432 | bytes 917532 | tf_op jit(solution)/shard_map/mul | solution.py:88
  8.5 2.7 collective-permute-start.1
  11.3 4.0 %collective-permute-start = (f32[32,1,128]{2,1,0:T(1,128)S(1)}, f32[32,1,128]{2,1,0:T(1,128)S(1)}, u32[]{:S(2)}, u32[]{:S(2)}) collective-permute-start(f32[32,1,128]{2,1,0:T(1,128)S(1)} %get-tuple-element.55), channel_id=1, source_target_pairs={{0,16},{16,32},{32,48},{48,64},{64,80},{80,96},{96,112},{1,17},{17... | collective-permute-start | bytes 49160 | tf_op jit(solution)/shard_map/ppermute | solution.py:25
  15.3 4.6 %collective-permute-start.2 = (f32[1,16,128]{2,1,0:T(8,128)S(1)}, f32[1,16,128]{2,1,0:T(8,128)S(1)}, u32[]{:S(2)}, u32[]{:S(2)}) collective-permute-start(f32[1,16,128]{2,1,0:T(8,128)S(1)} %get-tuple-element.58), channel_id=1, source_target_pairs={{1,0},{2,1},{3,2},{4,3},{5,4},{6,5},{7,6},{8,7},{9,8},{10,9},{11,1... | collective-permute-start | bytes 24584 | tf_op jit(solution)/shard_map/ppermute | solution.py:26
  19.9 1.9 collective-permute-start.3
  21.9 6.6 %collective-permute-done.3 = f32[1,16,128]{2,1,0:T(8,128)S(1)} collective-permute-done((f32[1,16,128]{2,1,0:T(8,128)S(1)}, f32[1,16,128]{2,1,0:T(8,128)S(1)}, u32[]{:S(2)}, u32[]{:S(2)}) %collective-permute-start.3) | collective-permute-done | bytes 8224 | tf_op jit(solution)/shard_map/ppermute | solution.py:25
  29.0 4.9 %multiply_reduce_fusion.1 = (f32[]{:T(128)}, f32[]{:T(128)}, f32[32,16,128]{2,1,0:T(8,128)S(1)}) fusion(pred[32,16,128]{2,1,0:T(8,128)(4,1)S(1)} %get-tuple-element.39, pred[32,16,128]{2,1,0:T(8,128)(4,1)S(1)} %get-tuple-element.38, f32[]{:T(128)} %bitcast.5, f32[]{:T(128)} %bitcast.4, f32[]{:T(128)} %bitcast.3, f32[32,16,128]{2,1,0:T(8,128)S(1)} %copy-done.6, ...), kind=kLoop, calls=%fused_computation.126 | loop fusion | flops 2031614 | bytes 1493024 | tf_op jit(solution)/shard_map/reduce_sum | solution.py:97
  33.9 10.3 %all-reduce.12 = (f32[]{:T(128)}, f32[]{:T(128)}) all-reduce(f32[]{:T(128)} %get-tuple-element.4, f32[]{:T(128)} %get-tuple-element.3), channel_id=1, replica_groups=mesh['size_0'=4,'size_1'=2,'gz_0'=2,'gz_1'=4,'gz_2'=2] {'size_0'}, use_global_device_ids=true, to_apply=%region_1.2 | all-reduce | flops 2 | bytes 16 | tf_op jit(solution)/shard_map/psum | solution.py:39
  44.2 5.6 %all-reduce.18 = (f32[]{:T(128)}, f32[]{:T(128)}) all-reduce(f32[]{:T(128)} %get-tuple-element.11, f32[]{:T(128)} %get-tuple-element.12), channel_id=1, replica_groups=mesh['size_0'=4,'size_1'=2,'gz_0'=2,'gz_1'=4,'gz_2'=2] {'size_1'}, use_global_device_ids=true, to_apply=%region_2.3 | all-reduce | flops 2 | bytes 16 | tf_op jit(solution)/shard_map/psum | solution.py:39
  49.9 7.1 %all-reduce.16 = (f32[]{:T(128)}, f32[]{:T(128)}) all-reduce(f32[]{:T(128)} %get-tuple-element.23, f32[]{:T(128)} %get-tuple-element.24), channel_id=1, replica_groups=mesh['size_0'=4,'size_1'=2,'gz_0'=2,'gz_1'=4,'gz_2'=2] {'gz_0'}, use_global_device_ids=true, to_apply=%region_3.4 | all-reduce | flops 2 | bytes 16 | tf_op jit(solution)/shard_map/psum | solution.py:39
  57.0 8.4 %all-reduce.10 = (f32[]{:T(128)}, f32[]{:T(128)}) all-reduce(f32[]{:T(128)} %get-tuple-element.19, f32[]{:T(128)} %get-tuple-element.20), channel_id=1, replica_groups=mesh['size_0'=4,'size_1'=2,'gz_0'=2,'gz_1'=4,'gz_2'=2] {'gz_1'}, use_global_device_ids=true, to_apply=%region_4.5 | all-reduce | flops 2 | bytes 16 | tf_op jit(solution)/shard_map/psum | solution.py:39
  65.5 3.2 %all-reduce.14 = (f32[]{:T(128)}, f32[]{:T(128)}) all-reduce(f32[]{:T(128)} %get-tuple-element.7, f32[]{:T(128)} %get-tuple-element.8), channel_id=1, replica_groups=mesh['size_0'=4,'size_1'=2,'gz_0'=2,'gz_1'=4,'gz_2'=2] {'gz_2'}, use_global_device_ids=true, to_apply=%region_5.6 | all-reduce | flops 2 | bytes 16 | tf_op jit(solution)/shard_map/psum | solution.py:39
  69.9 4.7 %fusion.38 = (f32[32,16,128]{2,1,0:T(8,128)S(1)}, f32[]{:T(128)}) fusion(pred[32,16,128]{2,1,0:T(8,128)(4,1)S(1)} %get-tuple-element.39, pred[32,16,128]{2,1,0:T(8,128)(4,1)S(1)} %get-tuple-element.38, f32[]{:T(128)} %bitcast.5, f32[]{:T(128)} %bitcast.4, f32[]{:T(128)} %bitcast.3, f32[32,16,128]{2,1,0:T(8,128)S(1)} %get-tuple-element.36, f32[]{:T(128)S(6)} %div.19, ...), kind=kLoop, calls=%fused_computation.129 | loop fusion | flops 917503 | bytes 917536 | tf_op jit(solution)/shard_map/mul | solution.py:88
  74.7 3.0 %collective-permute-start.5 = (f32[32,1,128]{2,1,0:T(1,128)S(1)}, f32[32,1,128]{2,1,0:T(1,128)S(1)}, u32[]{:S(2)}, u32[]{:S(2)}) collective-permute-start(f32[32,1,128]{2,1,0:T(1,128)S(1)} %get-tuple-element.52), channel_id=1, source_target_pairs={{16,0},{32,16},{48,32},{64,48},{80,64},{96,80},{112,96},{17,1},{33... | collective-permute-start | bytes 49160 | tf_op jit(solution)/shard_map/ppermute | solution.py:26
  77.7 3.7 %collective-permute-start.4 = (f32[32,1,128]{2,1,0:T(1,128)S(1)}, f32[32,1,128]{2,1,0:T(1,128)S(1)}, u32[]{:S(2)}, u32[]{:S(2)}) collective-permute-start(f32[32,1,128]{2,1,0:T(1,128)S(1)} %get-tuple-element.51), channel_id=1, source_target_pairs={{0,16},{16,32},{32,48},{48,64},{64,80},{80,96},{96,112},{1,17},{17... | collective-permute-start | bytes 49160 | tf_op jit(solution)/shard_map/ppermute | solution.py:25
  81.4 2.5 collective-permute-start.6
  84.0 1.9 collective-permute-start.7
  85.9 6.6 %collective-permute-done.7 = f32[1,16,128]{2,1,0:T(8,128)S(1)} collective-permute-done((f32[1,16,128]{2,1,0:T(8,128)S(1)}, f32[1,16,128]{2,1,0:T(8,128)S(1)}, u32[]{:S(2)}, u32[]{:S(2)}) %collective-permute-start.7) | collective-permute-done | bytes 8224 | tf_op jit(solution)/shard_map/ppermute | solution.py:25
  93.0 4.9 %fusion.28 = f32[]{:T(128)} fusion(f32[34,18,130]{2,1,0:T(8,128)S(1)} %select_maximum_fusion.8, f32[32,16,128]{2,1,0:T(8,128)S(1)} %get-tuple-element.49, f32[32,1,128]{2,1,0:T(1,128)S(1)} %collective-permute-done.4, f32[32,1,128]{2,1,0:T(1,128)S(1)} %collective-permute-done.5, f32[1,18,128]{2,1,0:T(8,128)S(1)} %pad.35, f32[1,18,128]{2,1,0:T(8,128)S(1)} %pad.34, ...), kind=kLoop, calls=%fused_computation.94 | loop fusion | flops 2031615 | bytes 1493024 | tf_op jit(solution)/shard_map/reduce_sum | solution.py:97
  97.9 9.7 %all-reduce.11 = (f32[]{:T(128)}, f32[]{:T(128)}) all-reduce(f32[]{:T(128)} %get-tuple-element.50, f32[]{:T(128)} %fusion.28), channel_id=1, replica_groups=mesh['size_0'=4,'size_1'=2,'gz_0'=2,'gz_1'=4,'gz_2'=2] {'size_0'}, use_global_device_ids=true, to_apply=%region_13.14 | all-reduce | flops 2 | bytes 16 | tf_op jit(solution)/shard_map/psum | solution.py:39
  107.6 5.6 %all-reduce.17 = (f32[]{:T(128)}, f32[]{:T(128)}) all-reduce(f32[]{:T(128)} %get-tuple-element.9, f32[]{:T(128)} %get-tuple-element.10), channel_id=1, replica_groups=mesh['size_0'=4,'size_1'=2,'gz_0'=2,'gz_1'=4,'gz_2'=2] {'size_1'}, use_global_device_ids=true, to_apply=%region_14.15 | all-reduce | flops 2 | bytes 16 | tf_op jit(solution)/shard_map/psum | solution.py:39
  113.2 7.1 %all-reduce.15 = (f32[]{:T(128)}, f32[]{:T(128)}) all-reduce(f32[]{:T(128)} %get-tuple-element.21, f32[]{:T(128)} %get-tuple-element.22), channel_id=1, replica_groups=mesh['size_0'=4,'size_1'=2,'gz_0'=2,'gz_1'=4,'gz_2'=2] {'gz_0'}, use_global_device_ids=true, to_apply=%region_15.16 | all-reduce | flops 2 | bytes 16 | tf_op jit(solution)/shard_map/psum | solution.py:39
  120.4 8.4 %all-reduce.9 = (f32[]{:T(128)}, f32[]{:T(128)}) all-reduce(f32[]{:T(128)} %get-tuple-element.17, f32[]{:T(128)} %get-tuple-element.18), channel_id=1, replica_groups=mesh['size_0'=4,'size_1'=2,'gz_0'=2,'gz_1'=4,'gz_2'=2] {'gz_1'}, use_global_device_ids=true, to_apply=%region_16.17 | all-reduce | flops 2 | bytes 16 | tf_op jit(solution)/shard_map/psum | solution.py:39
  128.8 3.1 %all-reduce.13 = (f32[]{:T(128)}, f32[]{:T(128)}) all-reduce(f32[]{:T(128)} %get-tuple-element.5, f32[]{:T(128)} %get-tuple-element.6), channel_id=1, replica_groups=mesh['size_0'=4,'size_1'=2,'gz_0'=2,'gz_1'=4,'gz_2'=2] {'gz_2'}, use_global_device_ids=true, to_apply=%region_17.18 | all-reduce | flops 2 | bytes 16 | tf_op jit(solution)/shard_map/psum | solution.py:39
  136.6 4.1 %multiply_add_fusion.6 = f32[32,16,128]{2,1,0:T(8,128)S(1)} fusion(f32[]{:T(128)S(6)} %div.21, f32[]{:T(128)S(6)} %div.23, f32[]{:T(128)S(6)} %div.19, pred[32,16,128]{2,1,0:T(8,128)(4,1)S(1)} %get-tuple-element.39, pred[32,16,128]{2,1,0:T(8,128)(4,1)S(1)} %get-tuple-element.38, f32[]{:T(128)} %bitcast.5, f32[]{:T(128)} %bitcast.4, f32[]{:T(128)} %bitcast.3, ...), kind=kLoop, calls=%fused_computation.123 | loop fusion | flops 1114112 | bytes 917540 | tf_op jit(solution)/shard_map/add | solution.py:171
  142.2 4.4 %all-to-all-start = ((f32[8,32,16,128]{3,2,1,0:T(8,128)}), f32[8,32,16,128]{3,2,1,0:T(8,128)}, u32[]{:S(2)}, u32[]{:S(2)}) async-start(f32[8,32,16,128]{3,2,1,0:T(8,128)} %broadcast_in_dim.57), calls=%async_computation | async-start | bytes 4194304 | tf_op jit(solution)/shard_map/all_to_all | solution.py:45
  146.6 3.3 %collective-permute-start.11 = (f32[1,128,128]{2,1,0:T(8,128)S(1)}, f32[1,128,128]{2,1,0:T(8,128)S(1)}, u32[]{:S(2)}, u32[]{:S(2)}) collective-permute-start(f32[1,128,128]{2,1,0:T(8,128)S(1)} %get-tuple-element.48), channel_id=1, source_target_pairs={{1,0},{2,1},{3,2},{4,3},{5,4},{6,5},{7,6},{8,7},{9,8},{10,9},{11,1... | collective-permute-start | bytes 196616 | tf_op jit(solution)/shard_map/ppermute | solution.py:69
  150.0 1.9 collective-permute-start.10
  153.9 5.6 %select_bitcast_fusion.1 = (f32[1,32,128,128]{3,2,1,0:T(8,128)}, pred[32,128,128]{2,1,0:T(8,128)(4,1)S(1)}, pred[32,128,128]{2,1,0:T(8,128)(4,1)S(1)}) fusion(f32[]{:T(128)} %bitcast.5, f32[]{:T(128)} %bitcast.4, f32[]{:T(128)} %bitcast.3, s32[32,128,128]{2,1,0:T(8,128)} %param.9), kind=kLoop, calls=%fused_computation.68 | loop fusion | flops 2097152 | bytes 5242892 | tf_op jit(solution)/shard_map/stack | solution.py:185
  159.4 3.6 %select_bitcast_fusion = f32[1,32,128,128]{3,2,1,0:T(8,128)} fusion(pred[32,128,128]{2,1,0:T(8,128)(4,1)S(1)} %get-tuple-element.35, pred[32,128,128]{2,1,0:T(8,128)(4,1)S(1)} %get-tuple-element.34, f32[]{:T(128)} %bitcast.13, f32[]{:T(128)} %bitcast.12, f32[]{:T(128)} %bitcast.11), kind=kLoop, calls=%fused_computation.67 | loop fusion | flops 1048576 | bytes 3145740 | tf_op jit(solution)/shard_map/stack | solution.py:185
  163.1 10.0 %all-to-all-done = f32[8,32,16,128]{3,2,1,0:T(8,128)} async-done(((f32[8,32,16,128]{3,2,1,0:T(8,128)}), f32[8,32,16,128]{3,2,1,0:T(8,128)}, u32[]{:S(2)}, u32[]{:S(2)}) %all-to-all-start) | async-done | bytes 2097184 | tf_op jit(solution)/shard_map/all_to_all | solution.py:45
  173.0 2.0 copy.12
  175.9 2.9 %collective-permute-start.9 = (f32[3,2,128,128]{3,2,1,0:T(8,128)S(1)}, f32[3,2,128,128]{3,2,1,0:T(8,128)S(1)}, u32[]{:S(2)}, u32[]{:S(2)}) collective-permute-start(f32[3,2,128,128]{3,2,1,0:T(8,128)S(1)} %get-tuple-element.44), channel_id=1, source_target_pairs={{1,0},{2,1},{3,2},{4,3},{5,4},{6,5},{7,6},{8,7},{9,8},{10,9},{11,1... | collective-permute-start | bytes 1179656 | tf_op jit(solution)/shard_map/ppermute | solution.py:69
  178.8 2.1 collective-permute-start.8
  181.0 4.3 %select_maximum_fusion.6 = f32[34,130,130]{2,1,0:T(8,128)} fusion(f32[1,128,128]{2,1,0:T(8,128)S(1)} %collective-permute-done.11, f32[32,128,128]{2,1,0:T(8,128)S(1)} %bitcast.57, f32[1,128,128]{2,1,0:T(8,128)S(1)} %collective-permute-done.10), kind=kLoop, calls=%fused_computation.18 | loop fusion | flops 8619000 | bytes 4526624 | tf_op jit(solution)/shard_map/concatenate | solution.py:65
  185.3 6.3 %collective-permute-done.8 = f32[3,2,128,128]{3,2,1,0:T(8,128)S(1)} collective-permute-done((f32[3,2,128,128]{3,2,1,0:T(8,128)S(1)}, f32[3,2,128,128]{3,2,1,0:T(8,128)S(1)}, u32[]{:S(2)}, u32[]{:S(2)}) %collective-permute-start.8) | collective-permute-done | bytes 393248 | tf_op jit(solution)/shard_map/ppermute | solution.py:67
  191.5 15.3 %select_maximum_fusion = f32[3,36,130,130]{3,2,1,0:T(8,128)} fusion(f32[3,2,128,128]{3,2,1,0:T(8,128)S(1)} %collective-permute-done.9, f32[3,2,128,128]{3,2,1,0:T(8,128)S(1)} %collective-permute-done.8, f32[1,32,128,128]{3,2,1,0:T(8,128)S(1)} %copy-done.2, f32[1,32,128,128]{3,2,1,0:T(8,128)S(1)} %copy-done.1, f32[1,32,128,128]{3,2,1,0:T(8,128)S(1)} %bitcast.60), kind=kLoop, calls=%fused_computation.4 | loop fusion | flops 38329200 | bytes 14378688 | tf_op jit(solution)/shard_map/concatenate | solution.py:65
  206.8 10.4 %slice_bitcast_fusion.2 = (f32[34,130,130]{2,1,0:T(8,128)}, f32[34,130,130]{2,1,0:T(8,128)}, f32[34,130,130]{2,1,0:T(8,128)}) fusion(f32[3,36,130,130]{3,2,1,0:T(8,128)} %select_maximum_fusion), kind=kLoop, calls=%fused_computation.21 | loop fusion | bytes 13790400 | tf_op jit(solution)/shard_map/squeeze | solution.py:118
  217.3 15.7 %multiply_add_fusion.1 = (f32[32,128,129]{2,1,0:T(8,128)}, f32[32,128,129]{2,1,0:T(8,128)}) fusion(f32[34,130,130]{2,1,0:T(8,128)} %select_maximum_fusion.6, f32[]{:T(128)} %bitcast.47, f32[34,130,130]{2,1,0:T(8,128)} %get-tuple-element.41, f32[34,130,130]{2,1,0:T(8,128)} %get-tuple-element.40, f32[]{:T(128)} %bitcast.44), kind=kLoop, calls=%fused_computation.30 | loop fusion | flops 6340608 | bytes 16908296 | tf_op jit(solution)/shard_map/add | solution.py:128
  233.0 5.0 %multiply_add_fusion.3 = (f32[32,129,128]{2,1,0:T(8,128)}, f32[32,129,128]{2,1,0:T(8,128)}) fusion(f32[34,130,130]{2,1,0:T(8,128)S(1)} %bitcast.56, f32[]{:T(128)} %bitcast.46, f32[34,130,130]{2,1,0:T(8,128)S(1)} %bitcast.54, f32[34,130,130]{2,1,0:T(8,128)S(1)} %bitcast.52, f32[]{:T(128)} %bitcast.43), kind=kLoop, calls=%fused_computation.36 | loop fusion | flops 6340608 | bytes 16908296 | tf_op jit(solution)/shard_map/add | solution.py:128
  238.1 9.3 %multiply_add_fusion.5 = (f32[33,128,128]{2,1,0:T(8,128)}, f32[33,128,128]{2,1,0:T(8,128)}) fusion(f32[1,128,128]{2,1,0:T(8,128)S(1)} %collective-permute-done.11, f32[32,128,128]{2,1,0:T(8,128)S(1)} %bitcast.58, f32[1,128,128]{2,1,0:T(8,128)S(1)} %collective-permute-done.10, f32[]{:T(128)} %bitcast.45, f32[34,130,130]{2,1,0:T(8,128)} %get-tuple-element.41, ...), kind=kLoop, calls=%fused_computation.46 | loop fusion | flops 7569408 | bytes 15204360 | tf_op jit(solution)/shard_map/add | solution.py:128
  247.4 9.7 %fusion.21 = (f32[1,32,128,128]{3,2,1,0:T(8,128)}, f32[32,128,128]{2,1,0:T(8,128)S(1)}) fusion(f32[1,32,128,128]{3,2,1,0:T(8,128)} %param.17, f32[34,130,130]{2,1,0:T(8,128)} %get-tuple-element.42, f32[1,32,128,128]{3,2,1,0:T(8,128)S(1)} %copy-done, f32[32,128,129]{2,1,0:T(8,128)} %get-tuple-element.31, f32[32,129,128]{2,1,0:T(8,128)} %get-tuple-element.29, ...), kind=kLoop, calls=%fused_computation.66 | loop fusion | flops 7340032 | bytes 23068672 | tf_op jit(solution)/shard_map/broadcast_in_dim | solution.py:197
  257.1 1.9 collective-permute-start.13
  259.0 2.9 %collective-permute-start.12 = (f32[1,128,128]{2,1,0:T(8,128)S(1)}, f32[1,128,128]{2,1,0:T(8,128)S(1)}, u32[]{:S(2)}, u32[]{:S(2)}) collective-permute-start(f32[1,128,128]{2,1,0:T(8,128)S(1)} %get-tuple-element.45), channel_id=1, source_target_pairs={{0,1},{1,2},{2,3},{3,4},{4,5},{5,6},{6,7},{7,8},{8,9},{9,10},{10,1... | collective-permute-start | bytes 196616 | tf_op jit(solution)/shard_map/ppermute | solution.py:67
  261.9 6.6 %collective-permute-done.12 = f32[1,128,128]{2,1,0:T(8,128)S(1)} collective-permute-done((f32[1,128,128]{2,1,0:T(8,128)S(1)}, f32[1,128,128]{2,1,0:T(8,128)S(1)}, u32[]{:S(2)}, u32[]{:S(2)}) %collective-permute-start.12) | collective-permute-done | bytes 65568 | tf_op jit(solution)/shard_map/ppermute | solution.py:67
  268.5 2.9 %select_maximum_fusion.4 = f32[34,130,130]{2,1,0:T(8,128)S(1)} fusion(f32[1,128,128]{2,1,0:T(8,128)S(1)} %collective-permute-done.13, f32[32,128,128]{2,1,0:T(8,128)S(1)} %get-tuple-element.26, f32[1,128,128]{2,1,0:T(8,128)S(1)} %collective-permute-done.12), kind=kLoop, calls=%fused_computation.15 | loop fusion | flops 8619000 | bytes 4526624 | tf_op jit(solution)/shard_map/concatenate | solution.py:65
  271.4 4.2 %multiply_add_fusion = f32[32,128,129]{2,1,0:T(8,128)} fusion(f32[34,130,130]{2,1,0:T(8,128)S(1)} %select_maximum_fusion.4, f32[32,128,129]{2,1,0:T(8,128)S(1)} %copy-done.3, f32[]{:T(128)} %bitcast.48), kind=kLoop, calls=%fused_computation.29 | loop fusion | flops 4227072 | bytes 8454148 | tf_op jit(solution)/shard_map/add | solution.py:128
  277.9 7.3 %fusion.13 = f32[1,32,128,128]{3,2,1,0:T(8,128)} fusion(f32[32,128,128]{2,1,0:T(8,128)S(1)} %get-tuple-element.26, f32[32,128,129]{2,1,0:T(8,128)} %multiply_add_fusion, f32[32,129,128]{2,1,0:T(8,128)S(1)} %multiply_add_fusion.2, f32[33,128,128]{2,1,0:T(8,128)S(1)} %multiply_add_fusion.4, f32[34,130,130]{2,1,0:T(8,128)} %get-tuple-element.42), kind=kLoop, calls=%fused_computation.52 | loop fusion | flops 4718592 | bytes 18874368 | tf_op jit(solution)/shard_map/broadcast_in_dim | solution.py:197
  (62 shorter events, 9.1 us)
Async XLA Ops:
  0.6 28.3 %copy-start.6 = (f32[32,16,128]{2,1,0:T(8,128)S(1)}, f32[32,16,128]{2,1,0:T(8,128)}, u32[]{:S(2)}) copy-start(f32[32,16,128]{2,1,0:T(8,128)} %param.10) | copy-start | bytes 786436
  8.5 20.0 %collective-permute-start.1 = (f32[32,1,128]{2,1,0:T(1,128)S(1)}, f32[32,1,128]{2,1,0:T(1,128)S(1)}, u32[]{:S(2)}, u32[]{:S(2)}) collective-permute-start(f32[32,1,128]{2,1,0:T(1,128)S(1)} %get-tuple-element.56), channel_id=1, source_target_pairs={{16,0},{32,16},{48,32},{64,48},{80,64},{96,80},{112,96},{17,1},{33... | collective-permute-start | bytes 49160 | tf_op jit(solution)/shard_map/ppermute | solution.py:26
  11.3 17.3 %collective-permute-start = (f32[32,1,128]{2,1,0:T(1,128)S(1)}, f32[32,1,128]{2,1,0:T(1,128)S(1)}, u32[]{:S(2)}, u32[]{:S(2)}) collective-permute-start(f32[32,1,128]{2,1,0:T(1,128)S(1)} %get-tuple-element.55), channel_id=1, source_target_pairs={{0,16},{16,32},{32,48},{48,64},{64,80},{80,96},{96,112},{1,17},{17... | collective-permute-start | bytes 49160 | tf_op jit(solution)/shard_map/ppermute | solution.py:25
  15.3 6.6 %collective-permute-start.2 = (f32[1,16,128]{2,1,0:T(8,128)S(1)}, f32[1,16,128]{2,1,0:T(8,128)S(1)}, u32[]{:S(2)}, u32[]{:S(2)}) collective-permute-start(f32[1,16,128]{2,1,0:T(8,128)S(1)} %get-tuple-element.58), channel_id=1, source_target_pairs={{1,0},{2,1},{3,2},{4,3},{5,4},{6,5},{7,6},{8,7},{9,8},{10,9},{11,1... | collective-permute-start | bytes 24584 | tf_op jit(solution)/shard_map/ppermute | solution.py:26
  19.9 8.6 %collective-permute-start.3 = (f32[1,16,128]{2,1,0:T(8,128)S(1)}, f32[1,16,128]{2,1,0:T(8,128)S(1)}, u32[]{:S(2)}, u32[]{:S(2)}) collective-permute-start(f32[1,16,128]{2,1,0:T(8,128)S(1)} %get-tuple-element.57), channel_id=1, source_target_pairs={{0,1},{1,2},{2,3},{3,4},{4,5},{5,6},{6,7},{7,8},{8,9},{9,10},{10,1... | collective-permute-start | bytes 24584 | tf_op jit(solution)/shard_map/ppermute | solution.py:25
  74.7 17.9 %collective-permute-start.5 = (f32[32,1,128]{2,1,0:T(1,128)S(1)}, f32[32,1,128]{2,1,0:T(1,128)S(1)}, u32[]{:S(2)}, u32[]{:S(2)}) collective-permute-start(f32[32,1,128]{2,1,0:T(1,128)S(1)} %get-tuple-element.52), channel_id=1, source_target_pairs={{16,0},{32,16},{48,32},{64,48},{80,64},{96,80},{112,96},{17,1},{33... | collective-permute-start | bytes 49160 | tf_op jit(solution)/shard_map/ppermute | solution.py:26
  77.7 14.9 %collective-permute-start.4 = (f32[32,1,128]{2,1,0:T(1,128)S(1)}, f32[32,1,128]{2,1,0:T(1,128)S(1)}, u32[]{:S(2)}, u32[]{:S(2)}) collective-permute-start(f32[32,1,128]{2,1,0:T(1,128)S(1)} %get-tuple-element.51), channel_id=1, source_target_pairs={{0,16},{16,32},{32,48},{48,64},{64,80},{80,96},{96,112},{1,17},{17... | collective-permute-start | bytes 49160 | tf_op jit(solution)/shard_map/ppermute | solution.py:25
  81.4 4.5 %collective-permute-start.6 = (f32[1,16,128]{2,1,0:T(8,128)S(1)}, f32[1,16,128]{2,1,0:T(8,128)S(1)}, u32[]{:S(2)}, u32[]{:S(2)}) collective-permute-start(f32[1,16,128]{2,1,0:T(8,128)S(1)} %get-tuple-element.54), channel_id=1, source_target_pairs={{1,0},{2,1},{3,2},{4,3},{5,4},{6,5},{7,6},{8,7},{9,8},{10,9},{11,1... | collective-permute-start | bytes 24584 | tf_op jit(solution)/shard_map/ppermute | solution.py:26
  84.0 8.6 %collective-permute-start.7 = (f32[1,16,128]{2,1,0:T(8,128)S(1)}, f32[1,16,128]{2,1,0:T(8,128)S(1)}, u32[]{:S(2)}, u32[]{:S(2)}) collective-permute-start(f32[1,16,128]{2,1,0:T(8,128)S(1)} %get-tuple-element.53), channel_id=1, source_target_pairs={{0,1},{1,2},{2,3},{3,4},{4,5},{5,6},{6,7},{7,8},{8,9},{9,10},{10,1... | collective-permute-start | bytes 24584 | tf_op jit(solution)/shard_map/ppermute | solution.py:25
  140.7 1.5 copy-start.7
  142.2 4.5 %copy-start = (f32[1,32,128,128]{3,2,1,0:T(8,128)S(1)}, f32[1,32,128,128]{3,2,1,0:T(8,128)}, u32[]{:S(2)}) copy-start(f32[1,32,128,128]{3,2,1,0:T(8,128)} %param.16) | copy-start | bytes 6291460
  142.2 11.0 %copy-start.8 = (f32[1,3]{1,0:T(1,128)S(1)}, f32[1,3]{1,0:T(1,128)}, u32[]{:S(2)}) copy-start(f32[1,3]{1,0:T(1,128)} %param.13) | copy-start | bytes 40
  142.2 30.9 %all-to-all-start = ((f32[8,32,16,128]{3,2,1,0:T(8,128)}), f32[8,32,16,128]{3,2,1,0:T(8,128)}, u32[]{:S(2)}, u32[]{:S(2)}) async-start(f32[8,32,16,128]{3,2,1,0:T(8,128)} %broadcast_in_dim.57), calls=%async_computation | async-start | bytes 4194304 | tf_op jit(solution)/shard_map/all_to_all | solution.py:45
  146.6 34.3 %collective-permute-start.11 = (f32[1,128,128]{2,1,0:T(8,128)S(1)}, f32[1,128,128]{2,1,0:T(8,128)S(1)}, u32[]{:S(2)}, u32[]{:S(2)}) collective-permute-start(f32[1,128,128]{2,1,0:T(8,128)S(1)} %get-tuple-element.48), channel_id=1, source_target_pairs={{1,0},{2,1},{3,2},{4,3},{5,4},{6,5},{7,6},{8,7},{9,8},{10,9},{11,1... | collective-permute-start | bytes 196616 | tf_op jit(solution)/shard_map/ppermute | solution.py:69
  150.0 31.0 %collective-permute-start.10 = (f32[1,128,128]{2,1,0:T(8,128)S(1)}, f32[1,128,128]{2,1,0:T(8,128)S(1)}, u32[]{:S(2)}, u32[]{:S(2)}) collective-permute-start(f32[1,128,128]{2,1,0:T(8,128)S(1)} %get-tuple-element.47), channel_id=1, source_target_pairs={{0,1},{1,2},{2,3},{3,4},{4,5},{5,6},{6,7},{7,8},{8,9},{9,10},{10,1... | collective-permute-start | bytes 196616 | tf_op jit(solution)/shard_map/ppermute | solution.py:67
  173.0 2.2 copy-start.1
  173.0 2.9 copy-start.2
  175.9 9.3 %collective-permute-start.9 = (f32[3,2,128,128]{3,2,1,0:T(8,128)S(1)}, f32[3,2,128,128]{3,2,1,0:T(8,128)S(1)}, u32[]{:S(2)}, u32[]{:S(2)}) collective-permute-start(f32[3,2,128,128]{3,2,1,0:T(8,128)S(1)} %get-tuple-element.44), channel_id=1, source_target_pairs={{1,0},{2,1},{3,2},{4,3},{5,4},{6,5},{7,6},{8,7},{9,8},{10,9},{11,1... | collective-permute-start | bytes 1179656 | tf_op jit(solution)/shard_map/ppermute | solution.py:69
  178.8 12.7 %collective-permute-start.8 = (f32[3,2,128,128]{3,2,1,0:T(8,128)S(1)}, f32[3,2,128,128]{3,2,1,0:T(8,128)S(1)}, u32[]{:S(2)}, u32[]{:S(2)}) collective-permute-start(f32[3,2,128,128]{3,2,1,0:T(8,128)S(1)} %get-tuple-element.43), channel_id=1, source_target_pairs={{0,1},{1,2},{2,3},{3,4},{4,5},{5,6},{6,7},{7,8},{8,9},{9,10},{10,1... | collective-permute-start | bytes 1179656 | tf_op jit(solution)/shard_map/ppermute | solution.py:67
  217.2 15.7 %slice-start = ((s8[4734976]{0:T(1024)(128)(4,1)}), s8[4194304]{0:T(1024)(128)(4,1)S(1)}, s32[]{:S(2)}) async-start(s8[4734976]{0:T(1024)(128)(4,1)} %bitcast.51), calls=%async_computation.1 | async-start | bytes 8388608
  217.2 15.7 %slice-start.2 = ((s8[4734976]{0:T(1024)(128)(4,1)}), s8[4194304]{0:T(1024)(128)(4,1)S(1)}, s32[]{:S(2)}) async-start(s8[4734976]{0:T(1024)(128)(4,1)} %bitcast.53), calls=%async_computation.3 | async-start | bytes 8388608
  217.2 15.7 %slice-start.4 = ((s8[4734976]{0:T(1024)(128)(4,1)}), s8[4194304]{0:T(1024)(128)(4,1)S(1)}, s32[]{:S(2)}) async-start(s8[4734976]{0:T(1024)(128)(4,1)} %bitcast.55), calls=%async_computation.5 | async-start | bytes 8388608
  217.2 15.8 %slice-start.1 = ((s8[4734976]{0:T(1024)(128)(4,1)}), s8[540672]{0:T(1024)(128)(4,1)S(1)}, s32[]{:S(2)}) async-start(s8[4734976]{0:T(1024)(128)(4,1)} %bitcast.51), calls=%async_computation.2 | async-start | bytes 1081344
  217.2 15.8 %slice-start.3 = ((s8[4734976]{0:T(1024)(128)(4,1)}), s8[540672]{0:T(1024)(128)(4,1)S(1)}, s32[]{:S(2)}) async-start(s8[4734976]{0:T(1024)(128)(4,1)} %bitcast.53), calls=%async_computation.4 | async-start | bytes 1081344
  217.2 15.8 %slice-start.5 = ((s8[4734976]{0:T(1024)(128)(4,1)}), s8[540672]{0:T(1024)(128)(4,1)S(1)}, s32[]{:S(2)}) async-start(s8[4734976]{0:T(1024)(128)(4,1)} %bitcast.55), calls=%async_computation.6 | async-start | bytes 1081344
  257.1 4.8 %collective-permute-start.13 = (f32[1,128,128]{2,1,0:T(8,128)S(1)}, f32[1,128,128]{2,1,0:T(8,128)S(1)}, u32[]{:S(2)}, u32[]{:S(2)}) collective-permute-start(f32[1,128,128]{2,1,0:T(8,128)S(1)} %get-tuple-element.46), channel_id=1, source_target_pairs={{1,0},{2,1},{3,2},{4,3},{5,4},{6,5},{7,6},{8,7},{9,8},{10,9},{11,1... | collective-permute-start | bytes 196616 | tf_op jit(solution)/shard_map/ppermute | solution.py:69
  259.0 12.4 %copy-start.3 = (f32[32,128,129]{2,1,0:T(8,128)S(1)}, f32[32,128,129]{2,1,0:T(8,128)}, u32[]{:S(2)}) copy-start(f32[32,128,129]{2,1,0:T(8,128)} %get-tuple-element.32) | copy-start | bytes 6340612
  259.0 9.5 %collective-permute-start.12 = (f32[1,128,128]{2,1,0:T(8,128)S(1)}, f32[1,128,128]{2,1,0:T(8,128)S(1)}, u32[]{:S(2)}, u32[]{:S(2)}) collective-permute-start(f32[1,128,128]{2,1,0:T(8,128)S(1)} %get-tuple-element.45), channel_id=1, source_target_pairs={{0,1},{1,2},{2,3},{3,4},{4,5},{5,6},{6,7},{7,8},{8,9},{9,10},{10,1... | collective-permute-start | bytes 196616 | tf_op jit(solution)/shard_map/ppermute | solution.py:67
  271.4 4.2 %copy-start.4 = (f32[32,129,128]{2,1,0:T(8,128)S(1)}, f32[32,129,128]{2,1,0:T(8,128)}, u32[]{:S(2)}) copy-start(f32[32,129,128]{2,1,0:T(8,128)} %get-tuple-element.30) | copy-start | bytes 6340612
  275.6 1.6 copy-start.5
where the time goes:
time: 286 us; the launch traced here: 285 us
  other arithmetic  109 us (38%)
  blocking collectives  68.7 us (24%)
  starting transfers between devices  44 us (15%)
  waiting for transfers between devices  36.1 us (13%)
  local copies, waits for them, and re-layouts  18.7 us (7%)
  between operations  8.34 us (3%)
    psum x10, blocking collectives, by_axis(): array = lax.psum(array, axis)  68.7 us
    add x6, other arithmetic, transport_step(): jnp.maximum(velocity, 0.0) * conc_low  36.1 us
    concatenate x3, other arithmetic, extended_2(): jnp.concatenate([lax.ppermute(tail, axis, [(i, (i + 1) % count) for i in...  22.5 us
    broadcast_in_dim x2, other arithmetic, local(): return (solution, conc[None], bound[None])  16.9 us
    ppermute x4, waiting for transfers between devices, extended(): lax.ppermute(last, axis, up)  13.3 us
    ppermute x4, starting transfers between devices, extended(): lax.ppermute(initial, axis, [(b, a) for a, b in up])  13 us
    ppermute x3, waiting for transfers between devices, extended_2(): lax.ppermute(tail, axis, [(i, (i + 1) % count) for i in range(ends)])  12.8 us
    ppermute x4, starting transfers between devices, extended(): lax.ppermute(last, axis, up)  11.5 us
  transfers between devices with their start and end apart: 15, of which 5 were waited for; matrix products, arithmetic and copies ran while one was open for 6% of the time, Pallas kernels for 0%

commit v1 on v0

v1 whole, which is shorter than its diff:
```python
import functools

import jax
import jax.numpy as jnp
from jax import lax
from jax.experimental import pallas as pl
from jax.experimental.pallas import tpu as pltpu
from jax.sharding import PartitionSpec as P

MESH = pl.DeviceIdType.MESH
TIME_STEP = 0.1
EDGE = 8


def select(labels, values):
    first, second = labels == 0, labels == 1
    return [jnp.where(first, v[0], jnp.where(second, v[1], v[2])) for v in values]


def two_sum(a, b):
    total = a + b
    part = total - a
    return total, (a - (total - part)) + (b - part)


def split(a):
    wide = 4097.0 * a
    high = wide - (wide - a)
    return high, a - high


def two_prod(a, b):
    product = a * b
    ah, al = split(a)
    bh, bl = split(b)
    return product, ((ah * bh - product) + ah * bl + al * bh) + al * bl


def pair_sub_product(x, a, b):
    p, e = two_prod(a[0], b[0])
    e = e + (a[0] * b[1] + a[1] * b[0])
    s, r = two_sum(x[0], -p)
    r = r + (x[1] - e)
    return two_sum(s, r)


def pair_ratio(x, y):
    q = x[0] / y[0]
    rest = pair_sub_product(x, (q, jnp.zeros_like(q)), y)
    return two_sum(q, (rest[0] + rest[1]) / y[0])


def scalar_tables(cond_ref, leak_ref):
    cond = [cond_ref[i] for i in range(3)]
    leak = [leak_ref[i] for i in range(3)]
    inverse = []
    for k, l in zip(cond, leak):
        inverse.append((1.0 / jnp.full((8, 128), 6.0 * k * k + l, jnp.float32))[0, 0])
    return cond, leak, inverse


def lane_neighbours(q, lane, ny):
    up = jnp.where(lane == ny - 1, 0.0, pltpu.roll(q, ny - 1, 1))
    down = jnp.where(lane == 0, 0.0, pltpu.roll(q, 1, 1))
    return up + down


def exchange_kernel(
    n_size, n_gz, cond_ref, leak_ref, vp, tissue, conc,
    slab, thalo, chalo, scal,
    ext, tex, qs, qv, ys, tile, red_size, red_gz, total_tile,
    local_sem, near_send, near_recv, block_send, block_recv, low_send, low_recv, high_send, high_recv,
    ring_send, ring_recv, grid_send, grid_recv,
):
    s, g = lax.axis_index("size"), lax.axis_index("gz")
    nz, bx, ny = vp.shape
    half = bx // 2
    nx = tissue.shape[1]

    ext[...] = jnp.zeros_like(ext)
    tex[...] = jnp.full_like(tex, 3)

    def remote(src, dst, send, recv, to_s, to_g):
        return pltpu.make_async_remote_copy(
            src_ref=src, dst_ref=dst, send_sem=send, recv_sem=recv,
            device_id={"size": to_s, "gz": to_g}, device_id_type=MESH)

    own_rows = pl.ds(pl.multiple_of(s * bx, 8), bx)

    barrier = pltpu.get_barrier_semaphore()

    def greet(to_s, to_g):
        pl.semaphore_signal(barrier, inc=1, device_id={"size": to_s, "gz": to_g}, device_id_type=MESH)

    greeted = 0
    for j in range(n_size):
        peer = lax.rem(s + j, n_size)
        for d in (0, 1, n_gz - 1):
            if j or d:
                greet(peer, lax.rem(g + d, n_gz))
                greeted += 1
    for j in range(2, n_gz - 1):
        greet(s, lax.rem(g + j, n_gz))
        greeted += 1

    inner = pltpu.make_async_copy(vp, ext.at[pl.ds(2, nz), pl.ds(half, bx)], local_sem.at[0])
    inner.start()
    own = pltpu.make_async_copy(vp, slab.at[pl.ds(3, nz), own_rows], local_sem.at[1])
    own.start()

    wide = bx + 2 * half

    def tissue_rows(which):
        if which == "low":
            return pl.ds(0, bx + half), pl.ds(half, bx + half)
        if which == "high":
            return pl.ds(nx - bx - half, bx + half), pl.ds(0, bx + half)
        return pl.ds(pl.multiple_of(s * bx - half, 8), wide), pl.ds(0, wide)

    cases = (("low", s == 0), ("high", s == n_size - 1), ("mid", (s > 0) & (s < n_size - 1)))

    def tex_copy(which):
        src, dst = tissue_rows(which)
        return pltpu.make_async_copy(tissue.at[:, src], tex.at[pl.ds(2, nz), dst], local_sem.at[2])

    for which, cond in cases:
        @pl.when(cond)
        def _(which=which):
            tex_copy(which).start()

    pl.semaphore_wait(barrier, greeted)

    lows, highs = pl.ds(0, half), pl.ds(half, half)
    above, below = pl.ds(half + bx, half), pl.ds(0, half)
    middle = pl.ds(half, bx)
    has_low, has_high = g > 0, g < n_gz - 1
    x_low, x_high = s > 0, s < n_size - 1
    near = [
        (x_high, x_low, vp.at[:, highs], ext.at[pl.ds(2, nz), below], 0, s + 1, g),
        (x_low, x_high, vp.at[:, lows], ext.at[pl.ds(2, nz), above], 1, s - 1, g),
        (has_high, has_low, vp.at[pl.ds(nz - 2, 2)], ext.at[pl.ds(0, 2), middle], 2, s, g + 1),
        (has_low, has_high, vp.at[pl.ds(0, 2)], ext.at[pl.ds(nz + 2, 2), middle], 3, s, g - 1),
        (x_high & has_high, x_low & has_low, vp.at[pl.ds(nz - 1, 1), highs], ext.at[pl.ds(1, 1), below], 4, s + 1, g + 1),
        (x_low & has_high, x_high & has_low, vp.at[pl.ds(nz - 1, 1), lows], ext.at[pl.ds(1, 1), above], 5, s - 1, g + 1),
        (x_high & has_low, x_low & has_high, vp.at[pl.ds(0, 1), highs], ext.at[pl.ds(nz + 2, 1), below], 6, s + 1, g - 1),
        (x_low & has_low, x_high & has_high, vp.at[pl.ds(0, 1), lows], ext.at[pl.ds(nz + 2, 1), above], 7, s - 1, g - 1),
    ]
    for which, cond in cases:
        src, dst = tissue_rows(which)
        near.append((has_high & cond, has_low & cond, tissue.at[pl.ds(nz - 2, 2), src], tex.at[pl.ds(0, 2), dst], 8, s, g + 1))
        near.append((has_low & cond, has_high & cond, tissue.at[pl.ds(0, 2), src], tex.at[pl.ds(nz + 2, 2), dst], 9, s, g - 1))
    late = [
        (has_high, has_low, tissue.at[pl.ds(nz - 3, 3)], thalo.at[pl.ds(0, 3)], 10, s, g + 1),
        (has_low, has_high, tissue.at[pl.ds(0, 3)], thalo.at[pl.ds(3, 3)], 11, s, g - 1),
        (has_high, has_low, conc.at[pl.ds(nz - 2, 2)], chalo.at[pl.ds(0, 2)], 12, s, g + 1),
        (has_low, has_high, conc.at[pl.ds(0, 2)], chalo.at[pl.ds(2, 2)], 13, s, g - 1),
    ]

    def start_all(copies):
        for cond, _, src, dst, i, to_s, to_g in copies:
            @pl.when(cond)
            def _(src=src, dst=dst, i=i, to_s=to_s, to_g=to_g):
                remote(src, dst, near_send.at[i], near_recv.at[i], to_s, to_g).start()

    def wait_all(copies):
        for sent, cond, src, dst, i, to_s, to_g in copies:
            @pl.when(cond)
            def _(src=src, dst=dst, i=i):
                remote(src, dst, near_send.at[i], near_recv.at[i], s, g).wait_recv()

            @pl.when(sent)
            def _(src=src, dst=dst, i=i):
                remote(src, dst, near_send.at[i], near_recv.at[i], s, g).wait_send()

    start_all(near)

    def block_copy(j):
        return remote(vp, slab.at[pl.ds(3, nz), own_rows], block_send.at[j], block_recv.at[s], lax.rem(s + j, n_size), g)

    order = sorted(range(1, n_size), key=lambda j: min(j, n_size - j))
    for j in order:
        block_copy(j).start()
    start_all(late)

    def low_copy(j):
        return remote(vp.at[pl.ds(nz - 3, 3)], slab.at[pl.ds(0, 3), own_rows], low_send.at[j], low_recv.at[s], lax.rem(s + j, n_size), g + 1)

    def high_copy(j):
        return remote(vp.at[pl.ds(0, 3)], slab.at[pl.ds(nz + 3, 3), own_rows], high_send.at[j], high_recv.at[s], lax.rem(s + j, n_size), g - 1)

    @pl.when(has_high)
    def _():
        for j in range(n_size):
            low_copy(j).start()

    @pl.when(has_low)
    def _():
        for j in range(n_size):
            high_copy(j).start()

    cond, leak, inverse = scalar_tables(cond_ref, leak_ref)
    first = [l * i for l, i in zip(leak, inverse)]
    second = [k * l * i for k, l, i in zip(cond, leak, inverse)]
    lane = lax.broadcasted_iota(jnp.int32, (wide, ny), 1)

    inner.wait()
    for which, c in cases:
        @pl.when(c)
        def _(which=which):
            tex_copy(which).wait()
    wait_all(near)

    def scale(e, _):
        (t2,) = select(tex[e], [second])
        qs[e] = t2 * ext[e]
        return 0

    lax.fori_loop(0, nz + 4, scale, 0)

    def stencil(ref, e):
        q = ref[e]
        total = ref[e - 1] + ref[e + 1] + pltpu.roll(q, 1, 0) + pltpu.roll(q, wide - 1, 0)
        return 6.0 * q - (total + lane_neighbours(q, lane, ny))

    def add_product(acc, a, b):
        p, e = two_prod(a, b)
        h, r = two_sum(acc[0], p)
        return h, acc[1] + (e + r)

    def apply(e):
        labels = tex[e]
        k, l, i, t1 = select(labels, [cond, leak, inverse, first])
        k = jnp.where(labels == 3, 0.0, k)
        field = ext[e]
        z = t1 * field
        az = l * z + k * stencil(qs, e)
        y = i * az
        qv[e] = k * y
        ys[e] = y
        return l * field, z, az, y

    def mine(x):
        return x[half:half + bx]

    def first_sums(e, accs):
        r0, z, az, y = (mine(x) for x in apply(e))
        return (add_product(accs[0], r0, z), add_product(accs[1], z, az), add_product(accs[2], y, az))

    apply(1)
    apply(nz + 2)
    zero = jnp.zeros((bx, ny), jnp.float32)
    sums = lax.fori_loop(2, nz + 2, first_sums, ((zero, zero),) * 3)

    def last_sum(e, acc):
        labels = tex[e]
        k, l = select(labels, [cond, leak])
        y = ys[e]
        ay = l * y + k * stencil(qv, e)
        return add_product(acc, mine(y), mine(ay))

    sums = (*sums, lax.fori_loop(2, nz + 2, last_sum, (zero, zero)))

    row = lax.broadcasted_iota(jnp.int32, (8, ny), 0)
    packed = jnp.zeros((8, ny), jnp.float32)
    for m, (h, l) in enumerate(sums):
        hs, ls = h[0:8], l[0:8]
        for r in range(8, bx, 8):
            hs, e = two_sum(hs, h[r:r + 8])
            ls = ls + l[r:r + 8] + e
        for shift in (4, 2, 1):
            hs, e = two_sum(hs, pltpu.roll(hs, shift, 0))
            ls = ls + pltpu.roll(ls, shift, 0) + e
        packed = jnp.where(row == m, hs, jnp.where(row == m + 4, ls, packed))
    tile[...] = packed

    def add_tiles(parts):
        total, errors = parts[0], jnp.zeros((8, ny), jnp.float32)
        for part in parts[1:]:
            total, e = two_sum(total, part)
            errors = errors + e
        return total + pltpu.roll(jnp.where(row < 4, errors, 0.0), 4, 0)

    def reduce(src, slots, index, count, axis, send, recv):
        for j in range(1, count):
            to = lax.rem(index + j, count)
            dev = (to, g) if axis == "size" else (s, to)
            remote(src, slots.at[index], send.at[j], recv.at[index], *dev).start()
        parts = []
        for j in range(1, count):
            frm = lax.rem(index + j, count)
            remote(src, slots.at[frm], send.at[j], recv.at[frm], s, g).wait()
        slots[index] = src[...]
        return add_tiles([slots[i] for i in range(count)])

    total_tile[...] = reduce(tile, red_size, s, n_size, "size", ring_send, ring_recv)
    total = reduce(total_tile, red_gz, g, n_gz, "gz", grid_send, grid_recv)

    errors = jnp.zeros_like(total)
    shift = ny // 2
    while shift:
        total, e = two_sum(total, pltpu.roll(total, shift, 1))
        errors = errors + pltpu.roll(errors, shift, 1) + e
        shift //= 2
    lower = pltpu.roll(total, 4, 0) + errors
    b = [(total[m:m + 1], lower[m:m + 1]) for m in range(4)]
    t = pair_ratio(b[1], b[0])
    v = pair_sub_product(b[2], t, b[1])
    w = pair_sub_product(pair_sub_product(b[3], t, b[2]), t, v)
    b0, b1, v, w, t = b[0][0], b[1][0], v[0], w[0], t[0]
    det = b1 * w - v * v
    x_part = b0 * w / det
    y_part = -(b0 * v) / det
    scal[...] = jnp.where(row == 0, x_part + y_part * (1.0 - t), -y_part)

    for j in range(1, n_size):
        block_copy(j).wait_send()
        frm = lax.rem(s + j, n_size)
        remote(vp, slab.at[pl.ds(3, nz), own_rows], block_send.at[j], block_recv.at[frm], s, g).wait_recv()
    own.wait()

    @pl.when(has_high)
    def _():
        for j in range(n_size):
            low_copy(j).wait_send()
            remote(vp.at[pl.ds(0, 3)], slab.at[pl.ds(nz + 3, 3), own_rows], high_send.at[j], high_recv.at[j], s, g).wait_recv()

    @pl.when(has_low)
    def _():
        for j in range(n_size):
            high_copy(j).wait_send()
            remote(vp.at[pl.ds(0, 3)], slab.at[pl.ds(0, 3), own_rows], low_send.at[j], low_recv.at[j], s, g).wait_recv()

    wait_all(late)


def exchange(n_size, n_gz, cond_table, leak_table, vp, tissue, conc):
    nz, bx, ny = vp.shape
    nx = tissue.shape[1]
    anywhere = pl.BlockSpec(memory_space=pl.ANY)
    scalars = pl.BlockSpec(memory_space=pltpu.SMEM)
    dma = pltpu.SemaphoreType.DMA
    return pl.pallas_call(
        functools.partial(exchange_kernel, n_size, n_gz),
        out_shape=(
            jax.ShapeDtypeStruct((nz + 6, nx, ny), jnp.float32),
            jax.ShapeDtypeStruct((6, nx, ny), jnp.int32),
            jax.ShapeDtypeStruct((4, nx, ny), jnp.float32),
            jax.ShapeDtypeStruct((8, ny), jnp.float32),
        ),
        in_specs=[scalars, scalars, anywhere, anywhere, anywhere],
        out_specs=(anywhere, anywhere, anywhere, pl.BlockSpec(memory_space=pltpu.VMEM)),
        scratch_shapes=[
            pltpu.VMEM((nz + 4, 2 * bx, ny), jnp.float32),
            pltpu.VMEM((nz + 4, 2 * bx, ny), jnp.int32),
            pltpu.VMEM((nz + 4, 2 * bx, ny), jnp.float32),
            pltpu.VMEM((nz + 4, 2 * bx, ny), jnp.float32),
            pltpu.VMEM((nz + 4, 2 * bx, ny), jnp.float32),
            pltpu.VMEM((8, ny), jnp.float32),
            pltpu.VMEM((n_size, 8, ny), jnp.float32),
            pltpu.VMEM((n_gz, 8, ny), jnp.float32),
            pltpu.VMEM((8, ny), jnp.float32),
            dma((3,)),
            dma((14,)), dma((14,)),
            dma((n_size,)), dma((n_size,)),
            dma((n_size,)), dma((n_size,)),
            dma((n_size,)), dma((n_size,)),
            dma((n_size,)), dma((n_size,)),
            dma((n_gz,)), dma((n_gz,)),
        ],
        compiler_params=pltpu.CompilerParams(collective_id=0, has_side_effects=True, vmem_limit_bytes=16 << 20),
        name="exchange",
    )(cond_table, leak_table, vp, tissue, conc)


def transport_kernel(
    n_gz, cond_ref, leak_ref, bind_ref, hinder_ref, diffuse_ref, scal, slab, tissue, thalo, conc, chalo, bound,
    pressure, free_out, bound_out,
    vps, tis, c0, c1, bnd, out, qs, ps, ks, coef_z, wx, coefs, sems, out_sems, pressure_sem,
):
    s, g = lax.axis_index("size"), lax.axis_index("gz")
    nz, nx, ny = conc.shape
    bx = pressure.shape[1]
    rows = 32 if nx % 32 == 0 else nx
    chunk = 8
    n_chunks = nz // chunk
    has_low, has_high = g > 0, g < n_gz - 1
    inside = pl.ds(EDGE, nx)

    def chunk_copies(i):
        z0 = i * chunk
        return [
            pltpu.make_async_copy(slab.at[pl.ds(z0 + 3, chunk)], vps.at[pl.ds(z0 + 3, chunk)], sems.at[i, 0]),
            pltpu.make_async_copy(tissue.at[pl.ds(z0, chunk)], tis.at[pl.ds(z0 + 3, chunk)], sems.at[i, 1]),
            pltpu.make_async_copy(conc.at[pl.ds(z0, chunk)], c0.at[pl.ds(z0 + 2, chunk), inside], sems.at[i, 2]),
            pltpu.make_async_copy(bound.at[pl.ds(z0, chunk)], bnd.at[pl.ds(z0, chunk)], sems.at[i, 3]),
        ]

    def halo_copies(high):
        i, h, v, c = n_chunks + int(high), 3 * high, nz + 3 if high else 0, nz + 2 if high else 0
        return [
            pltpu.make_async_copy(slab.at[pl.ds(v, 3)], vps.at[pl.ds(v, 3)], sems.at[i, 0]),
            pltpu.make_async_copy(thalo.at[pl.ds(h, 3)], tis.at[pl.ds(v, 3)], sems.at[i, 1]),
            pltpu.make_async_copy(chalo.at[pl.ds(2 * high, 2)], c0.at[pl.ds(c, 2), inside], sems.at[i, 2]),
        ]

    def each(copies, what):
        for copy in copies:
            getattr(copy, what)()

    @pl.when(has_low)
    def _():
        each(halo_copies(False), "start")

    for i in range(n_chunks):
        each(chunk_copies(i), "start")

    @pl.when(has_high)
    def _():
        each(halo_copies(True), "start")

    edge_rows = jnp.zeros((EDGE, ny), jnp.float32)

    def clear(i, _):
        for ref in (c0, c1, qs, ps, ks):
            ref[i, pl.ds(0, EDGE), :] = edge_rows
            ref[i, pl.ds(EDGE + nx, EDGE), :] = edge_rows
        return 0

    lax.fori_loop(0, nz + 4, clear, 0)
    for i in (nz + 4, nz + 5):
        qs[i, pl.ds(0, EDGE), :] = edge_rows
        qs[i, pl.ds(EDGE + nx, EDGE), :] = edge_rows
    wx[pl.ds(0, EDGE), :] = edge_rows

    def blank(high):
        v, c = (nz + 3, nz + 2) if high else (0, 0)
        for i in range(3):
            vps[v + i] = jnp.zeros((nx, ny), jnp.float32)
            tis[v + i] = jnp.zeros((nx, ny), jnp.int32)
        for i in range(2):
            c0[c + i, inside, :] = jnp.zeros((nx, ny), jnp.float32)

    @pl.when(g == 0)
    def _():
        blank(False)

    @pl.when(g == n_gz - 1)
    def _():
        blank(True)

    cond, leak, inverse = scalar_tables(cond_ref, leak_ref)
    x_part, y_part = scal[0, 0], scal[1, 0]
    hinder = TIME_STEP * hinder_ref[0]
    diffuse = TIME_STEP * diffuse_ref[0]
    rate = [TIME_STEP * bind_ref[0, i] for i in range(3)]
    second = [k * l * i for k, l, i in zip(cond, leak, inverse)]
    z_part = [x_part * l * i for l, i in zip(leak, inverse)]
    n_part = [y_part * k * i for k, i in zip(cond, inverse)]
    lane = lax.broadcasted_iota(jnp.int32, (rows, ny), 1)
    first_lane, last_lane = lane == 0, lane == ny - 1
    diffuse_low = jnp.where(first_lane, 0.0, diffuse)
    diffuse_high = jnp.where(last_lane, 0.0, diffuse)
    starts = range(0, nx, rows)

    def scale(p):
        for r in starts:
            block = pl.ds(r, rows)
            (t2,) = select(tis[p + 3, block, :], [second])
            qs[p + 3, pl.ds(EDGE + r, rows), :] = t2 * vps[p + 3, block, :]

    def press(p):
        for r in starts:
            block = pl.ds(r, rows)
            here = pl.ds(EDGE + r, rows)
            k, zp, npart = select(tis[p + 3, block, :], [cond, z_part, n_part])
            q = qs[p + 3, here, :]
            total = qs[p + 2, here, :] + qs[p + 4, here, :]
            total = total + qs[p + 3, pl.ds(EDGE + r - 1, rows), :] + qs[p + 3, pl.ds(EDGE + r + 1, rows), :]
            total = total + jnp.where(first_lane, 0.0, pltpu.roll(q, 1, 1)) + jnp.where(last_lane, 0.0, pltpu.roll(q, ny - 1, 1))
            ps[p + 2, here, :] = zp * vps[p + 3, block, :] + npart * total
            ks[p + 2, here, :] = k

        @pl.when(((p < 0) & (g == 0)) | ((p >= nz) & (g == n_gz - 1)))
        def _():
            ks[p + 2, inside, :] = jnp.zeros((nx, ny), jnp.float32)

    def z_face(p, r):
        here = pl.ds(EDGE + r, rows)
        k, press_here = ks[p + 2, here, :] * hinder, ps[p + 2, here, :]
        w = k * ks[p + 3, here, :] * (press_here - ps[p + 3, here, :])
        return k, press_here, w

    def faces(p, slot, before):
        for r in starts:
            block = pl.ds(r, rows)
            here = pl.ds(EDGE + r, rows)
            k, press_here, w = z_face(p, r)
            a = jnp.maximum(w, 0.0) + diffuse
            b = a - w
            coef_z[slot, 0, block, :] = a
            coef_z[slot, 1, block, :] = b
            after = pl.ds(EDGE + r + 1, rows)
            w_x = k * ks[p + 2, after, :] * (press_here - ps[p + 2, after, :])
            wx[here, :] = w_x
            a_x = jnp.maximum(w_x, 0.0) + diffuse
            b_x = a_x - w_x
            w_low = wx[pl.ds(EDGE + r - 1, rows), :]
            a_x_low = jnp.maximum(w_low, 0.0) + diffuse
            b_x_low = a_x_low - w_low
            k_here = ks[p + 2, here, :]
            w_y = k * pltpu.roll(k_here, ny - 1, 1) * (press_here - pltpu.roll(press_here, ny - 1, 1))
            w_y = jnp.where(last_lane, 0.0, w_y)
            up = jnp.maximum(w_y, 0.0)
            a_y = up + diffuse
            b_y = (up - w_y) + diffuse_high
            w_low = pltpu.roll(w_y, 1, 1)
            up = jnp.maximum(w_low, 0.0)
            a_y_low = up + diffuse_low
            b_y_low = (up - w_low) + diffuse
            (bind,) = select(tis[p + 3, block, :], [rate])
            centre = (a + a_x) + (a_y + b_x_low) + (b_y_low + coef_z[before, 1, block, :]) + bind
            coefs[slot, 0, block, :] = 1.0 - centre
            coefs[slot, 1, block, :] = a_x_low
            coefs[slot, 2, block, :] = b_x
            coefs[slot, 3, block, :] = a_y_low
            coefs[slot, 4, block, :] = b_y

    def advance(src, p, slot, before, r):
        block = pl.ds(r, rows)
        here = pl.ds(EDGE + r, rows)
        c = src[p + 2, here, :]
        value = coefs[slot, 0, block, :] * c
        value = value + coef_z[slot, 1, block, :] * src[p + 3, here, :] + coef_z[before, 0, block, :] * src[p + 1, here, :]
        value = value + coefs[slot, 1, block, :] * src[p + 2, pl.ds(EDGE + r - 1, rows), :]
        value = value + coefs[slot, 2, block, :] * src[p + 2, pl.ds(EDGE + r + 1, rows), :]
        value = value + coefs[slot, 3, block, :] * pltpu.roll(c, 1, 1)
        value = value + coefs[slot, 4, block, :] * pltpu.roll(c, ny - 1, 1)
        return c, value

    def first_step(p, slot, before):
        for r in starts:
            _, value = advance(c0, p, slot, before, r)
            c1[p + 2, pl.ds(EDGE + r, rows), :] = value

        @pl.when(((p < 0) & (g == 0)) | ((p >= nz) & (g == n_gz - 1)))
        def _():
            c1[p + 2, inside, :] = jnp.zeros((nx, ny), jnp.float32)

    def second_step(p, slot, before):
        for r in starts:
            block = pl.ds(r, rows)
            c, value = advance(c1, p, slot, before, r)
            out[p, block, :] = value
            (bind,) = select(tis[p + 3, block, :], [rate])
            bnd[p, block, :] = bnd[p, block, :] + bind * (c0[p + 2, pl.ds(EDGE + r, rows), :] + c)

    def out_copies(i):
        z0 = pl.ds(i * chunk, chunk)
        return [
            pltpu.make_async_copy(out.at[z0], free_out.at[z0], out_sems.at[i, 0]),
            pltpu.make_async_copy(bnd.at[z0], bound_out.at[z0], out_sems.at[i, 1]),
        ]

    @pl.when(has_low)
    def _():
        each(halo_copies(False), "wait")

    each(chunk_copies(0), "wait")

    for p in range(-3, 1):
        scale(p)
    for p in (-2, -1):
        press(p)
    for r in starts:
        w = z_face(-2, r)[2]
        a = jnp.maximum(w, 0.0) + diffuse
        coef_z[1, 0, pl.ds(r, rows), :] = a
        coef_z[1, 1, pl.ds(r, rows), :] = a - w
    scale(1)
    press(0)
    faces(-1, 2, 1)
    first_step(-1, 2, 1)

    def body(p, _):
        slot, before, older = lax.rem(p, 3), lax.rem(p + 2, 3), lax.rem(p + 1, 3)
        group = lax.div(p + 2, chunk)

        @pl.when((lax.rem(p + 2, chunk) == 0) & (group < n_chunks))
        def _():
            each(chunk_copies(group), "wait")

        @pl.when((p == nz - 2) & has_high)
        def _():
            each(halo_copies(True), "wait")

        scale(p + 2)
        press(p + 1)
        faces(p, slot, before)
        first_step(p, slot, before)

        @pl.when(p > 0)
        def _():
            second_step(p - 1, before, older)

        @pl.when((p > 0) & (lax.rem(p, chunk) == 0))
        def _():
            each(out_copies(lax.div(p, chunk) - 1), "start")

        return 0

    lax.fori_loop(0, nz + 1, body, 0)
    own = pltpu.make_async_copy(
        ps.at[pl.ds(2, nz), pl.ds(pl.multiple_of(EDGE + s * bx, 8), bx)], pressure, pressure_sem)
    own.start()
    for i in range(n_chunks):
        each(out_copies(i), "wait")
    own.wait()


def transport(n_gz, bx, cond_table, leak_table, bind_table, hindrance, diffusivity, scal, slab, tissue, thalo, conc, chalo, bound):
    nz, nx, ny = conc.shape
    anywhere = pl.BlockSpec(memory_space=pl.ANY)
    scalars = pl.BlockSpec(memory_space=pltpu.SMEM)
    wide = nx + 2 * EDGE
    f32 = jnp.float32
    dma = pltpu.SemaphoreType.DMA
    n_chunks = nz // 8
    return pl.pallas_call(
        functools.partial(transport_kernel, n_gz),
        out_shape=(
            jax.ShapeDtypeStruct((nz, bx, ny), f32),
            jax.ShapeDtypeStruct((nz, nx, ny), f32),
            jax.ShapeDtypeStruct((nz, nx, ny), f32),
        ),
        in_specs=[scalars] * 5 + [pl.BlockSpec(memory_space=pltpu.VMEM)] + [anywhere] * 6,
        out_specs=(anywhere, anywhere, anywhere),
        scratch_shapes=[
            pltpu.VMEM((nz + 6, nx, ny), f32),
            pltpu.VMEM((nz + 6, nx, ny), jnp.int32),
            pltpu.VMEM((nz + 4, wide, ny), f32),
            pltpu.VMEM((nz + 4, wide, ny), f32),
            pltpu.VMEM((nz, nx, ny), f32),
            pltpu.VMEM((nz, nx, ny), f32),
            pltpu.VMEM((nz + 6, wide, ny), f32),
            pltpu.VMEM((nz + 4, wide, ny), f32),
            pltpu.VMEM((nz + 4, wide, ny), f32),
            pltpu.VMEM((3, 2, nx, ny), f32),
            pltpu.VMEM((wide, ny), f32),
            pltpu.VMEM((3, 5, nx, ny), f32),
            dma((n_chunks + 2, 4)),
            dma((n_chunks, 2)),
            dma,
        ],
        compiler_params=pltpu.CompilerParams(vmem_limit_bytes=40 << 20),
        name="transport",
    )(cond_table, leak_table, bind_table, hindrance, diffusivity, scal, slab, tissue, thalo, conc, chalo, bound)


def solution(mesh):
    n_size, n_gz = mesh.shape["size"], mesh.shape["gz"]

    def local(tissue, vessel_pressure, cond_table, leak_table, bind_table, hindrance, diffusivity, free_conc, bound_conc):
        conc, bound = free_conc[0], bound_conc[0]
        slab, thalo, chalo, scal = exchange(n_size, n_gz, cond_table, leak_table, vessel_pressure, tissue, conc)
        pressure, free, held = transport(
            n_gz, vessel_pressure.shape[1], cond_table, leak_table, bind_table, hindrance, diffusivity,
            scal, slab, tissue, thalo, conc, chalo, bound)
        return pressure, free[None], held[None]

    return jax.shard_map(
        local,
        mesh=mesh,
        in_specs=(
            P("gz", None, None), P("gz", "size", None), P(), P(), P("size", None), P("size"), P("size"),
            P("size", "gz", None, None), P("size", "gz", None, None),
        ),
        out_specs=(P("gz", "size", None), P("size", "gz", None, None), P("size", "gz", None, None)),
        check_vma=False,
    )
```

time: 286 us -> 84.2 us (0.29)
  other arithmetic: 109 us -> 0 us
  Pallas kernels: 0 us -> 73.9 us
  blocking collectives: 68.7 us -> 0 us
  starting transfers between devices: 44 us -> 0 us
  waiting for transfers between devices: 36.1 us -> 0 us
  local copies, waits for them, and re-layouts: 18.7 us -> 7.04 us
  between operations: 8.34 us -> 2.01 us
    pallas_call x0 -> x2, Pallas kernels: none -> 73.9 us  [the longest x1 54.8 us: exchange(): pl.pallas_call(functools.partial(exchange_kernel, n_size, n_gz), out_shap...]
    psum x10 -> x0, blocking collectives: 68.7 us -> none  [by_axis(): array = lax.psum(array, axis)]
    add x7 -> x0, other arithmetic: 40.2 us -> none  [the longest x6 36.1 us: transport_step(): jnp.maximum(velocity, 0.0) * conc_low]
    ppermute x14 -> x0, starting transfers between devices: 39.5 us -> none  [the longest x4 13 us: extended(): lax.ppermute(initial, axis, [(b, a) for a, b in up])]
    ppermute x14 -> x0, waiting for transfers between devices: 26.1 us -> none  [the longest x4 13.3 us: extended(): lax.ppermute(last, axis, up)]
    concatenate x5 -> x0, other arithmetic: 23.4 us -> none  [the longest x3 22.5 us: extended_2(): jnp.concatenate([lax.ppermute(tail, axis, [(i, (i + 1) % count) for i in...]
    broadcast_in_dim x2 -> x0, other arithmetic: 16.9 us -> none  [local(): return (solution, conc[None], bound[None])]
    squeeze x1 -> x0, local copies, waits for them, and re-layouts: 10.4 us -> none  [transport_step(): cond_line = along_line(fields_pad[1], along_dim)]
  transfers between devices with their start and end apart: 15 -> 0, of which waited for: 5 -> 0; matrix products, arithmetic and copies ran while one was open for 6% -> 0% of each run, Pallas kernels for 0% -> 0%
where the time goes in v1:
time: 84.2 us; the launch traced here: 82.9 us
  Pallas kernels  73.9 us (88%)
  local copies, waits for them, and re-layouts  7.04 us (8%)
  between operations  2.01 us (2%)
    pallas_call x1, Pallas kernels, exchange(): pl.pallas_call(functools.partial(exchange_kernel, n_size, n_gz), out_shap...  54.8 us
    pallas_call x1, Pallas kernels, transport(): pl.pallas_call(functools.partial(transport_kernel, n_gz), out_shape=(jax....  19.1 us
    unnamed x22, local copies, waits for them, and re-layouts  7.04 us

profile of v1, /device:TPU:6, one launch (start us, length us, event | category | flops | bytes accessed | tf_op | source)
XLA Modules:
  0.0 82.9 jit_solution(905614749809021425)
XLA Ops:
  1.9 0.0 copy-start
  1.9 1.6 %copy-done = s32[32,128,128]{2,1,0:T(8,128)S(1)} copy-done((s32[32,128,128]{2,1,0:T(8,128)S(1)}, s32[32,128,128]{2,1,0:T(8,128)}, u32[]{:S(2)}) %copy-start) | copy-done | bytes 2097176
  3.5 0.0 copy-start.2
  3.5 1.6 %copy-done.2 = f32[1,32,128,128]{3,2,1,0:T(8,128)S(1)} copy-done((f32[1,32,128,128]{3,2,1,0:T(8,128)S(1)}, f32[1,32,128,128]{3,2,1,0:T(8,128)}, u32[]{:S(2)}) %copy-start.2) | copy-done | bytes 2097176
  5.1 0.0 copy-start.5
  5.1 0.9 %copy-done.5 = f32[32,16,128]{2,1,0:T(8,128)S(1)} copy-done((f32[32,16,128]{2,1,0:T(8,128)S(1)}, f32[32,16,128]{2,1,0:T(8,128)}, u32[]{:S(2)}) %copy-start.5) | copy-done | bytes 262168
  6.1 0.0 copy-start.6
  6.1 0.7 copy-done.6
  6.7 0.0 copy-start.8
  6.7 0.7 copy-done.8
  7.4 0.0 copy-start.1
  7.4 0.0 copy-start.3
  7.4 0.0 copy-start.7
  7.4 0.0 copy-start.9
  7.4 0.0 copy-start.10
  7.4 54.8 %exchange.1 = (f32[38,128,128]{2,1,0:T(8,128)S(1)}, s32[6,128,128]{2,1,0:T(8,128)S(1)}, f32[4,128,128]{2,1,0:T(8,128)S(1)}, f32[8,128]{1,0:T(8,128)S(1)}) custom-call(f32[3]{0:T(128)S(1)} %copy-done.6, f32[3]{0:T(128)S(1)} %copy-done.8, f32[32,16,128]{2,1,0:T(8,128)S(1)} %copy-done.5, s32[32,128,128]{2,1,0:T(8,128)S(1)} %copy-done, f32[32,128,128]{2,1,0:T(8,128)S(1)} %bitcast.4), custom_call_target="tpu_custom_call" | custom-call | tf_op jit(solution)/shard_map/exchange/pallas_call | solution.py:342
  62.2 0.0 copy-done.1
  62.2 0.0 copy-done.3
  62.2 0.0 copy-done.7
  62.2 0.0 copy-done.9
  62.2 0.0 copy-done.10
  62.2 0.0 copy-start.4
  62.2 1.6 %copy-done.4 = f32[1,32,128,128]{3,2,1,0:T(8,128)S(1)} copy-done((f32[1,32,128,128]{3,2,1,0:T(8,128)S(1)}, f32[1,32,128,128]{3,2,1,0:T(8,128)}, u32[]{:S(2)}) %copy-start.4) | copy-done | bytes 2097176
  63.8 19.1 %transport.1 = (f32[32,16,128]{2,1,0:T(8,128)}, f32[32,128,128]{2,1,0:T(8,128)}, f32[32,128,128]{2,1,0:T(8,128)}) custom-call(f32[3]{0:T(128)S(1)} %copy-done.7, f32[3]{0:T(128)S(1)} %copy-done.9, f32[1,3]{1,0:T(1,128)S(1)} %copy-done.10, f32[1]{0:T(128)S(6)} %copy.12.hinder_ref, f32[1]{0:T(128)S(6)} %copy.13.diffuse_ref, ...), custom_call_target="tpu_custom_call" | custom-call | tf_op jit(solution)/shard_map/transport/pallas_call | solution.py:628
Async XLA Ops:
  1.9 1.6 %copy-start = (s32[32,128,128]{2,1,0:T(8,128)S(1)}, s32[32,128,128]{2,1,0:T(8,128)}, u32[]{:S(2)}) copy-start(s32[32,128,128]{2,1,0:T(8,128)} %tissue.3) | copy-start | bytes 6291460
  3.5 1.6 %copy-start.2 = (f32[1,32,128,128]{3,2,1,0:T(8,128)S(1)}, f32[1,32,128,128]{3,2,1,0:T(8,128)}, u32[]{:S(2)}) copy-start(f32[1,32,128,128]{3,2,1,0:T(8,128)} %param.16) | copy-start | bytes 6291460
  5.1 0.9 %copy-start.5 = (f32[32,16,128]{2,1,0:T(8,128)S(1)}, f32[32,16,128]{2,1,0:T(8,128)}, u32[]{:S(2)}) copy-start(f32[32,16,128]{2,1,0:T(8,128)} %vp.1) | copy-start | bytes 786436
  6.1 0.7 copy-start.6
  6.7 0.7 copy-start.8
  7.4 54.8 %copy-start.1 = (s32[32,128,128]{2,1,0:T(8,128)S(1)}, s32[32,128,128]{2,1,0:T(8,128)}, u32[]{:S(2)}) copy-start(s32[32,128,128]{2,1,0:T(8,128)} %tissue.3) | copy-start | bytes 6291460
  7.4 54.8 %copy-start.3 = (f32[1,32,128,128]{3,2,1,0:T(8,128)S(1)}, f32[1,32,128,128]{3,2,1,0:T(8,128)}, u32[]{:S(2)}) copy-start(f32[1,32,128,128]{3,2,1,0:T(8,128)} %param.16) | copy-start | bytes 6291460
  7.4 54.8 %copy-start.7 = (f32[3]{0:T(128)S(1)}, f32[3]{0:T(128)}, u32[]{:S(2)}) copy-start(f32[3]{0:T(128)} %cond_ref.3) | copy-start | bytes 40
  7.4 54.8 %copy-start.9 = (f32[3]{0:T(128)S(1)}, f32[3]{0:T(128)}, u32[]{:S(2)}) copy-start(f32[3]{0:T(128)} %leak_ref.3) | copy-start | bytes 40
  7.4 54.8 %copy-start.10 = (f32[1,3]{1,0:T(1,128)S(1)}, f32[1,3]{1,0:T(1,128)}, u32[]{:S(2)}) copy-start(f32[1,3]{1,0:T(1,128)} %bind_ref.1) | copy-start | bytes 40
  62.2 1.6 %copy-start.4 = (f32[1,32,128,128]{3,2,1,0:T(8,128)S(1)}, f32[1,32,128,128]{3,2,1,0:T(8,128)}, u32[]{:S(2)}) copy-start(f32[1,32,128,128]{3,2,1,0:T(8,128)} %param.17) | copy-start | bytes 6291460

commit v2 on v1

--- a/solution.py
+++ b/solution.py
@@ -10,6 +10,12 @@
 MESH = pl.DeviceIdType.MESH
 TIME_STEP = 0.1
 EDGE = 8
+CHUNKS = 4
+
+
+def each(copies, what):
+    for copy in copies:
+        getattr(copy, what)()
 
 
 def select(labels, values):
@@ -68,8 +74,8 @@
 def exchange_kernel(
     n_size, n_gz, cond_ref, leak_ref, vp, tissue, conc,
     slab, thalo, chalo, scal,
-    ext, tex, qs, qv, ys, tile, red_size, red_gz, total_tile,
-    local_sem, near_send, near_recv, block_send, block_recv, low_send, low_recv, high_send, high_recv,
+    ext, tex, qs, qv, ys, packed_out, packed_in, tile, red_size, red_gz, total_tile,
+    local_sem, near_send, near_recv, block_send, block_recv,
     ring_send, ring_recv, grid_send, grid_recv,
 ):
     s, g = lax.axis_index("size"), lax.axis_index("gz")
@@ -95,7 +101,7 @@
     greeted = 0
     for j in range(n_size):
         peer = lax.rem(s + j, n_size)
-        for d in (0, 1, n_gz - 1):
+        for d in ((0,) if 1 < j < n_size - 1 else (0, 1, n_gz - 1)):
             if j or d:
                 greet(peer, lax.rem(g + d, n_gz))
                 greeted += 1
@@ -128,6 +134,14 @@
         def _(which=which):
             tex_copy(which).start()
 
+    inner.wait()
+
+    def pack(e, _):
+        for i, r in enumerate((half, half + 1, half + bx - 2, half + bx - 1)):
+            packed_out[i, pl.ds(e, 1), :] = ext[e + 2, pl.ds(r, 1), :]
+        return 0
+
+    lax.fori_loop(0, nz, pack, 0, unroll=4)
     pl.semaphore_wait(barrier, greeted)
 
     lows, highs = pl.ds(0, half), pl.ds(half, half)
@@ -136,8 +150,8 @@
     has_low, has_high = g > 0, g < n_gz - 1
     x_low, x_high = s > 0, s < n_size - 1
     near = [
-        (x_high, x_low, vp.at[:, highs], ext.at[pl.ds(2, nz), below], 0, s + 1, g),
-        (x_low, x_high, vp.at[:, lows], ext.at[pl.ds(2, nz), above], 1, s - 1, g),
+        (x_high, x_low, packed_out.at[pl.ds(2, 2)], packed_in.at[pl.ds(0, 2)], 0, s + 1, g),
+        (x_low, x_high, packed_out.at[pl.ds(0, 2)], packed_in.at[pl.ds(2, 2)], 1, s - 1, g),
         (has_high, has_low, vp.at[pl.ds(nz - 2, 2)], ext.at[pl.ds(0, 2), middle], 2, s, g + 1),
         (has_low, has_high, vp.at[pl.ds(0, 2)], ext.at[pl.ds(nz + 2, 2), middle], 3, s, g - 1),
         (x_high & has_high, x_low & has_low, vp.at[pl.ds(nz - 1, 1), highs], ext.at[pl.ds(1, 1), below], 4, s + 1, g + 1),
@@ -174,41 +188,90 @@
 
     start_all(near)
 
-    def block_copy(j):
-        return remote(vp, slab.at[pl.ds(3, nz), own_rows], block_send.at[j], block_recv.at[s], lax.rem(s + j, n_size), g)
-
-    order = sorted(range(1, n_size), key=lambda j: min(j, n_size - j))
-    for j in order:
-        block_copy(j).start()
+    n_z = n_size // 2
+    z, x = lax.div(s, 2), lax.rem(s, 2)
+    z_up, z_down, z_far = lax.rem(z + 1, n_z), lax.rem(z + n_z - 1, n_z), lax.rem(z + 2, n_z)
+    across = 2 * z + 1 - x
+    up, down, far = 2 * z_up + x, 2 * z_down + x, 2 * z_far + x
+    up_across, down_across, far_across = 2 * z_up + 1 - x, 2 * z_down + 1 - x, 2 * z_far + 1 - x
+    depth = nz // CHUNKS
+    part = depth // 2
+    order = [0, CHUNKS - 1, *range(1, CHUNKS - 1)]
+
+    def piece(block, c, kind, to, first=0, count=depth, own=False):
+        planes = pl.ds(3 + c * depth + first, count)
+        where = pl.ds(pl.multiple_of(block * bx, 8), bx)
+        src = vp.at[pl.ds(c * depth + first, count)] if own else slab.at[planes, where]
+        return remote(src, slab.at[planes, where], block_send.at[kind, c], block_recv.at[kind, c], to, g)
+
+    def own_pieces(c):
+        return [piece(s, c, 0, across, own=True), piece(s, c, 1, up, own=True), piece(s, c, 2, down, own=True)]
+
+    def from_across(c):
+        return [piece(across, c, 3, up), piece(across, c, 4, down)]
+
+    def from_down(c):
+        return [piece(down, c, 5, up, 0, part)]
+
+    def from_up(c):
+        return [piece(up, c, 6, down, part, depth - part)]
+
+    def from_far(c):
+        return [piece(far, c, 7, across)]
+
+    def hand_on(c):
+        piece(across, c, 0, s).wait_recv()
+        each(from_across(c), "start")
+        piece(down, c, 1, s).wait_recv()
+        each(from_down(c), "start")
+        piece(up, c, 2, s).wait_recv()
+        each(from_up(c), "start")
+
+    def hand_far(c):
+        piece(far, c, 5, s, 0, part).wait_recv()
+        piece(far, c, 6, s, part, depth - part).wait_recv()
+        each(from_far(c), "start")
+
+    def finish(c):
+        piece(down_across, c, 3, s).wait_recv()
+        piece(up_across, c, 4, s).wait_recv()
+        piece(far_across, c, 7, s).wait_recv()
+
+    for c in order:
+        each(own_pieces(c), "start")
     start_all(late)
 
-    def low_copy(j):
-        return remote(vp.at[pl.ds(nz - 3, 3)], slab.at[pl.ds(0, 3), own_rows], low_send.at[j], low_recv.at[s], lax.rem(s + j, n_size), g + 1)
-
-    def high_copy(j):
-        return remote(vp.at[pl.ds(0, 3)], slab.at[pl.ds(nz + 3, 3), own_rows], high_send.at[j], high_recv.at[s], lax.rem(s + j, n_size), g - 1)
-
-    @pl.when(has_high)
-    def _():
-        for j in range(n_size):
-            low_copy(j).start()
-
-    @pl.when(has_low)
-    def _():
-        for j in range(n_size):
-            high_copy(j).start()
+    edges = [
+        (has_high, has_low, slab.at[pl.ds(nz, 3)], slab.at[pl.ds(0, 3)], 14, s, g + 1),
+        (has_low, has_high, slab.at[pl.ds(3, 3)], slab.at[pl.ds(nz + 3, 3)], 15, s, g - 1),
+    ]
 
     cond, leak, inverse = scalar_tables(cond_ref, leak_ref)
     first = [l * i for l, i in zip(leak, inverse)]
     second = [k * l * i for k, l, i in zip(cond, leak, inverse)]
     lane = lax.broadcasted_iota(jnp.int32, (wide, ny), 1)
 
-    inner.wait()
     for which, c in cases:
         @pl.when(c)
         def _(which=which):
             tex_copy(which).wait()
     wait_all(near)
+
+    def unpack(low):
+        def rows_in(e, _):
+            for i in range(2):
+                r = half - 2 + i if low else half + bx + i
+                ext[e + 2, pl.ds(r, 1), :] = packed_in[i if low else 2 + i, pl.ds(e, 1), :]
+            return 0
+        lax.fori_loop(0, nz, rows_in, 0, unroll=4)
+
+    @pl.when(x_low)
+    def _():
+        unpack(True)
+
+    @pl.when(x_high)
+    def _():
+        unpack(False)
 
     def scale(e, _):
         (t2,) = select(tex[e], [second])
@@ -280,20 +343,30 @@
             errors = errors + e
         return total + pltpu.roll(jnp.where(row < 4, errors, 0.0), 4, 0)
 
-    def reduce(src, slots, index, count, axis, send, recv):
+    def reduce(src, slots, index, count, axis, send, recv, between):
         for j in range(1, count):
             to = lax.rem(index + j, count)
             dev = (to, g) if axis == "size" else (s, to)
             remote(src, slots.at[index], send.at[j], recv.at[index], *dev).start()
-        parts = []
+        between()
         for j in range(1, count):
             frm = lax.rem(index + j, count)
             remote(src, slots.at[frm], send.at[j], recv.at[frm], s, g).wait()
         slots[index] = src[...]
         return add_tiles([slots[i] for i in range(count)])
 
-    total_tile[...] = reduce(tile, red_size, s, n_size, "size", ring_send, ring_recv)
-    total = reduce(total_tile, red_gz, g, n_gz, "gz", grid_send, grid_recv)
+    def first_half():
+        for c in order[:CHUNKS // 2]:
+            hand_on(c)
+
+    def second_half():
+        for c in order[:CHUNKS // 2]:
+            hand_far(c)
+        for c in order[CHUNKS // 2:]:
+            hand_on(c)
+
+    total_tile[...] = reduce(tile, red_size, s, n_size, "size", ring_send, ring_recv, first_half)
+    total = reduce(total_tile, red_gz, g, n_gz, "gz", grid_send, grid_recv, second_half)
 
     errors = jnp.zeros_like(total)
     shift = ny // 2
@@ -312,25 +385,18 @@
     y_part = -(b0 * v) / det
     scal[...] = jnp.where(row == 0, x_part + y_part * (1.0 - t), -y_part)
 
-    for j in range(1, n_size):
-        block_copy(j).wait_send()
-        frm = lax.rem(s + j, n_size)
-        remote(vp, slab.at[pl.ds(3, nz), own_rows], block_send.at[j], block_recv.at[frm], s, g).wait_recv()
     own.wait()
-
-    @pl.when(has_high)
-    def _():
-        for j in range(n_size):
-            low_copy(j).wait_send()
-            remote(vp.at[pl.ds(0, 3)], slab.at[pl.ds(nz + 3, 3), own_rows], high_send.at[j], high_recv.at[j], s, g).wait_recv()
-
-    @pl.when(has_low)
-    def _():
-        for j in range(n_size):
-            high_copy(j).wait_send()
-            remote(vp.at[pl.ds(0, 3)], slab.at[pl.ds(0, 3), own_rows], low_send.at[j], low_recv.at[j], s, g).wait_recv()
-
+    for c in order[:2]:
+        finish(c)
+    start_all(edges)
+    for c in order[CHUNKS // 2:]:
+        hand_far(c)
+    for c in order[2:]:
+        finish(c)
+    for c in order:
+        each(own_pieces(c) + from_across(c) + from_down(c) + from_up(c) + from_far(c), "wait_send")
     wait_all(late)
+    wait_all(edges)
 
 
 def exchange(n_size, n_gz, cond_table, leak_table, vp, tissue, conc):
@@ -338,6 +404,7 @@
     nx = tissue.shape[1]
     anywhere = pl.BlockSpec(memory_space=pl.ANY)
     scalars = pl.BlockSpec(memory_space=pltpu.SMEM)
+    hbm = pl.BlockSpec(memory_space=pltpu.HBM)
     dma = pltpu.SemaphoreType.DMA
     return pl.pallas_call(
         functools.partial(exchange_kernel, n_size, n_gz),
@@ -347,7 +414,7 @@
             jax.ShapeDtypeStruct((4, nx, ny), jnp.float32),
             jax.ShapeDtypeStruct((8, ny), jnp.float32),
         ),
-        in_specs=[scalars, scalars, anywhere, anywhere, anywhere],
+        in_specs=[scalars, scalars, hbm, hbm, hbm],
         out_specs=(anywhere, anywhere, anywhere, pl.BlockSpec(memory_space=pltpu.VMEM)),
         scratch_shapes=[
             pltpu.VMEM((nz + 4, 2 * bx, ny), jnp.float32),
@@ -355,19 +422,19 @@
             pltpu.VMEM((nz + 4, 2 * bx, ny), jnp.float32),
             pltpu.VMEM((nz + 4, 2 * bx, ny), jnp.float32),
             pltpu.VMEM((nz + 4, 2 * bx, ny), jnp.float32),
+            pltpu.VMEM((4, nz, ny), jnp.float32),
+            pltpu.VMEM((4, nz, ny), jnp.float32),
             pltpu.VMEM((8, ny), jnp.float32),
             pltpu.VMEM((n_size, 8, ny), jnp.float32),
             pltpu.VMEM((n_gz, 8, ny), jnp.float32),
             pltpu.VMEM((8, ny), jnp.float32),
             dma((3,)),
-            dma((14,)), dma((14,)),
-            dma((n_size,)), dma((n_size,)),
-            dma((n_size,)), dma((n_size,)),
-            dma((n_size,)), dma((n_size,)),
+            dma((16,)), dma((16,)),
+            dma((8, CHUNKS)), dma((8, CHUNKS)),
             dma((n_size,)), dma((n_size,)),
             dma((n_gz,)), dma((n_gz,)),
         ],
-        compiler_params=pltpu.CompilerParams(collective_id=0, has_side_effects=True, vmem_limit_bytes=16 << 20),
+        compiler_params=pltpu.CompilerParams(collective_id=0, has_side_effects=True, vmem_limit_bytes=60 << 20),
         name="exchange",
     )(cond_table, leak_table, vp, tissue, conc)
 
@@ -402,10 +469,6 @@
             pltpu.make_async_copy(thalo.at[pl.ds(h, 3)], tis.at[pl.ds(v, 3)], sems.at[i, 1]),
             pltpu.make_async_copy(chalo.at[pl.ds(2 * high, 2)], c0.at[pl.ds(c, 2), inside], sems.at[i, 2]),
         ]
-
-    def each(copies, what):
-        for copy in copies:
-            getattr(copy, what)()
 
     @pl.when(has_low)
     def _():
@@ -621,6 +684,7 @@
     nz, nx, ny = conc.shape
     anywhere = pl.BlockSpec(memory_space=pl.ANY)
     scalars = pl.BlockSpec(memory_space=pltpu.SMEM)
+    hbm = pl.BlockSpec(memory_space=pltpu.HBM)
     wide = nx + 2 * EDGE
     f32 = jnp.float32
     dma = pltpu.SemaphoreType.DMA
@@ -632,7 +696,7 @@
             jax.ShapeDtypeStruct((nz, nx, ny), f32),
             jax.ShapeDtypeStruct((nz, nx, ny), f32),
         ),
-        in_specs=[scalars] * 5 + [pl.BlockSpec(memory_space=pltpu.VMEM)] + [anywhere] * 6,
+        in_specs=[scalars] * 5 + [pl.BlockSpec(memory_space=pltpu.VMEM), anywhere, hbm, anywhere, hbm, anywhere, hbm],
         out_specs=(anywhere, anywhere, anywhere),
         scratch_shapes=[
             pltpu.VMEM((nz + 6, nx, ny), f32),
@@ -651,7 +715,7 @@
             dma((n_chunks, 2)),
             dma,
         ],
-        compiler_params=pltpu.CompilerParams(vmem_limit_bytes=40 << 20),
+        compiler_params=pltpu.CompilerParams(vmem_limit_bytes=60 << 20),
         name="transport",
     )(cond_table, leak_table, bind_table, hindrance, diffusivity, scal, slab, tissue, thalo, conc, chalo, bound)
 

time: 84.2 us -> 60.1 us (0.71)
  the two profiles are of different devices: /device:TPU:6 before, /device:TPU:1 now
where the time goes in v2:
time: 60.1 us; the launch traced here: 59.9 us
  Pallas kernels  58 us (97%)
  between operations  1.93 us (3%)
    pallas_call x1, Pallas kernels, exchange(): pl.pallas_call(functools.partial(exchange_kernel, n_size, n_gz), out_shap...  39 us
    pallas_call x1, Pallas kernels, transport(): pl.pallas_call(functools.partial(transport_kernel, n_gz), out_shape=(jax....  19 us

profile of v2, /device:TPU:1, one launch (start us, length us, event | category | flops | bytes accessed | tf_op | source)
XLA Modules:
  0.0 59.9 jit_solution(2855766953799639949)
XLA Ops:
  1.9 39.0 %exchange.1 = (f32[38,128,128]{2,1,0:T(8,128)}, s32[6,128,128]{2,1,0:T(8,128)}, f32[4,128,128]{2,1,0:T(8,128)}, f32[8,128]{1,0:T(8,128)}) custom-call(f32[3]{0:T(128)} %cond_ref.3, f32[3]{0:T(128)} %leak_ref.3, f32[32,16,128]{2,1,0:T(8,128)} %vp.1, s32[32,128,128]{2,1,0:T(8,128)} %tissue.3, f32[32,128,128]{2,1,0:T(8,128)} %bitcast.4), custom_call_target="tpu_custom_call" | custom-call | tf_op jit(solution)/shard_map/exchange/pallas_call | solution.py:409
  40.9 19.0 %transport.1 = (f32[32,16,128]{2,1,0:T(8,128)}, f32[32,128,128]{2,1,0:T(8,128)}, f32[32,128,128]{2,1,0:T(8,128)}) custom-call(f32[3]{0:T(128)} %cond_ref.3, f32[3]{0:T(128)} %leak_ref.3, f32[1,3]{1,0:T(1,128)} %bind_ref.1, f32[1]{0:T(128)S(6)} %copy.12.hinder_ref, f32[1]{0:T(128)S(6)} %copy.13.diffuse_ref, f32[8,128]{1,0:T(8,128)} %get-tuple-element.10.scal, ...), custom_call_target="tpu_custom_call" | custom-call | tf_op jit(solution)/shard_map/transport/pallas_call | solution.py:692

commit v3 on v2

--- a/solution.py
+++ b/solution.py
@@ -278,7 +278,8 @@
         qs[e] = t2 * ext[e]
         return 0
 
-    lax.fori_loop(0, nz + 4, scale, 0)
+    lax.fori_loop(0, nz + 4, scale, 0, unroll=4)
+    hand_on(order[0])
 
     def stencil(ref, e):
         q = ref[e]
@@ -286,9 +287,8 @@
         return 6.0 * q - (total + lane_neighbours(q, lane, ny))
 
     def add_product(acc, a, b):
-        p, e = two_prod(a, b)
-        h, r = two_sum(acc[0], p)
-        return h, acc[1] + (e + r)
+        h, r = two_sum(acc[0], a[1] * b[1])
+        return h, acc[1] + ((a[1] * b[2] + a[2] * b[0]) + r)
 
     def apply(e):
         labels = tex[e]
@@ -303,7 +303,8 @@
         return l * field, z, az, y
 
     def mine(x):
-        return x[half:half + bx]
+        x = x[half:half + bx]
+        return (x, *split(x))
 
     def first_sums(e, accs):
         r0, z, az, y = (mine(x) for x in apply(e))
@@ -312,7 +313,9 @@
     apply(1)
     apply(nz + 2)
     zero = jnp.zeros((bx, ny), jnp.float32)
-    sums = lax.fori_loop(2, nz + 2, first_sums, ((zero, zero),) * 3)
+    sums = lax.fori_loop(2, nz + 2, first_sums, ((zero, zero),) * 3, unroll=2)
+    hand_on(order[1])
+    hand_far(order[0])
 
     def last_sum(e, acc):
         labels = tex[e]
@@ -321,7 +324,7 @@
         ay = l * y + k * stencil(qv, e)
         return add_product(acc, mine(y), mine(ay))
 
-    sums = (*sums, lax.fori_loop(2, nz + 2, last_sum, (zero, zero)))
+    sums = (*sums, lax.fori_loop(2, nz + 2, last_sum, (zero, zero), unroll=4))
 
     row = lax.broadcasted_iota(jnp.int32, (8, ny), 0)
     packed = jnp.zeros((8, ny), jnp.float32)
@@ -347,23 +350,20 @@
         for j in range(1, count):
             to = lax.rem(index + j, count)
             dev = (to, g) if axis == "size" else (s, to)
-            remote(src, slots.at[index], send.at[j], recv.at[index], *dev).start()
+            remote(src, slots.at[index], send, recv, *dev).start()
         between()
-        for j in range(1, count):
-            frm = lax.rem(index + j, count)
-            remote(src, slots.at[frm], send.at[j], recv.at[frm], s, g).wait()
+        arrived = slots.at[pl.ds(0, count - 1)]
+        remote(arrived, arrived, send, recv, s, g).wait()
         slots[index] = src[...]
         return add_tiles([slots[i] for i in range(count)])
 
     def first_half():
-        for c in order[:CHUNKS // 2]:
-            hand_on(c)
+        hand_on(order[2])
+        hand_far(order[1])
 
     def second_half():
-        for c in order[:CHUNKS // 2]:
-            hand_far(c)
-        for c in order[CHUNKS // 2:]:
-            hand_on(c)
+        hand_on(order[3])
+        hand_far(order[2])
 
     total_tile[...] = reduce(tile, red_size, s, n_size, "size", ring_send, ring_recv, first_half)
     total = reduce(total_tile, red_gz, g, n_gz, "gz", grid_send, grid_recv, second_half)
@@ -389,8 +389,7 @@
     for c in order[:2]:
         finish(c)
     start_all(edges)
-    for c in order[CHUNKS // 2:]:
-        hand_far(c)
+    hand_far(order[3])
     for c in order[2:]:
         finish(c)
     for c in order:
@@ -404,6 +403,7 @@
     nx = tissue.shape[1]
     anywhere = pl.BlockSpec(memory_space=pl.ANY)
     scalars = pl.BlockSpec(memory_space=pltpu.SMEM)
+    vmem = pl.BlockSpec(memory_space=pltpu.VMEM)
     hbm = pl.BlockSpec(memory_space=pltpu.HBM)
     dma = pltpu.SemaphoreType.DMA
     return pl.pallas_call(
@@ -431,10 +431,9 @@
             dma((3,)),
             dma((16,)), dma((16,)),
             dma((8, CHUNKS)), dma((8, CHUNKS)),
-            dma((n_size,)), dma((n_size,)),
-            dma((n_gz,)), dma((n_gz,)),
+            dma, dma, dma, dma,
         ],
-        compiler_params=pltpu.CompilerParams(collective_id=0, has_side_effects=True, vmem_limit_bytes=60 << 20),
+        compiler_params=pltpu.CompilerParams(collective_id=0, has_side_effects=True, vmem_limit_bytes=16 << 20),
         name="exchange",
     )(cond_table, leak_table, vp, tissue, conc)
 
@@ -442,12 +441,12 @@
 def transport_kernel(
     n_gz, cond_ref, leak_ref, bind_ref, hinder_ref, diffuse_ref, scal, slab, tissue, thalo, conc, chalo, bound,
     pressure, free_out, bound_out,
-    vps, tis, c0, c1, bnd, out, qs, ps, ks, coef_z, wx, coefs, sems, out_sems, pressure_sem,
+    c0, c1, bnd, out, qs, ps, ks, flow_x, flow, coefs, sems, out_sems, pressure_sem,
 ):
     s, g = lax.axis_index("size"), lax.axis_index("gz")
     nz, nx, ny = conc.shape
     bx = pressure.shape[1]
-    rows = 32 if nx % 32 == 0 else nx
+    rows = 64 if nx % 64 == 0 else nx
     chunk = 8
     n_chunks = nz // chunk
     has_low, has_high = g > 0, g < n_gz - 1
@@ -456,18 +455,14 @@
     def chunk_copies(i):
         z0 = i * chunk
         return [
-            pltpu.make_async_copy(slab.at[pl.ds(z0 + 3, chunk)], vps.at[pl.ds(z0 + 3, chunk)], sems.at[i, 0]),
-            pltpu.make_async_copy(tissue.at[pl.ds(z0, chunk)], tis.at[pl.ds(z0 + 3, chunk)], sems.at[i, 1]),
-            pltpu.make_async_copy(conc.at[pl.ds(z0, chunk)], c0.at[pl.ds(z0 + 2, chunk), inside], sems.at[i, 2]),
-            pltpu.make_async_copy(bound.at[pl.ds(z0, chunk)], bnd.at[pl.ds(z0, chunk)], sems.at[i, 3]),
+            pltpu.make_async_copy(conc.at[pl.ds(z0, chunk)], c0.at[pl.ds(z0 + 2, chunk), inside], sems.at[i, 0]),
+            pltpu.make_async_copy(bound.at[pl.ds(z0, chunk)], bnd.at[pl.ds(z0, chunk)], sems.at[i, 1]),
         ]
 
     def halo_copies(high):
-        i, h, v, c = n_chunks + int(high), 3 * high, nz + 3 if high else 0, nz + 2 if high else 0
+        i, c = n_chunks + int(high), nz + 2 if high else 0
         return [
-            pltpu.make_async_copy(slab.at[pl.ds(v, 3)], vps.at[pl.ds(v, 3)], sems.at[i, 0]),
-            pltpu.make_async_copy(thalo.at[pl.ds(h, 3)], tis.at[pl.ds(v, 3)], sems.at[i, 1]),
-            pltpu.make_async_copy(chalo.at[pl.ds(2 * high, 2)], c0.at[pl.ds(c, 2), inside], sems.at[i, 2]),
+            pltpu.make_async_copy(chalo.at[pl.ds(2 * high, 2)], c0.at[pl.ds(c, 2), inside], sems.at[i, 0]),
         ]
 
     @pl.when(has_low)
@@ -493,13 +488,11 @@
     for i in (nz + 4, nz + 5):
         qs[i, pl.ds(0, EDGE), :] = edge_rows
         qs[i, pl.ds(EDGE + nx, EDGE), :] = edge_rows
-    wx[pl.ds(0, EDGE), :] = edge_rows
+    for i in range(2):
+        flow_x[i, pl.ds(0, EDGE), :] = edge_rows
 
     def blank(high):
-        v, c = (nz + 3, nz + 2) if high else (0, 0)
-        for i in range(3):
-            vps[v + i] = jnp.zeros((nx, ny), jnp.float32)
-            tis[v + i] = jnp.zeros((nx, ny), jnp.int32)
+        c = nz + 2 if high else 0
         for i in range(2):
             c0[c + i, inside, :] = jnp.zeros((nx, ny), jnp.float32)
 
@@ -525,54 +518,71 @@
     diffuse_high = jnp.where(last_lane, 0.0, diffuse)
     starts = range(0, nx, rows)
 
+    def kind(p, block):
+        if isinstance(p, int) and p < 0:
+            return thalo[p + 3, block, :]
+        if isinstance(p, int) and p >= nz:
+            return thalo[p - nz + 3, block, :]
+        return tissue[p, block, :]
+
+    def field(p, block):
+        value = slab[p + 3, block, :]
+        if isinstance(p, int) and (p < 0 or p >= nz):
+            value = jnp.where(has_low if p < 0 else has_high, value, 0.0)
+        return value
+
     def scale(p):
         for r in starts:
             block = pl.ds(r, rows)
-            (t2,) = select(tis[p + 3, block, :], [second])
-            qs[p + 3, pl.ds(EDGE + r, rows), :] = t2 * vps[p + 3, block, :]
+            (t2,) = select(kind(p, block), [second])
+            qs[p + 3, pl.ds(EDGE + r, rows), :] = t2 * field(p, block)
 
     def press(p):
         for r in starts:
             block = pl.ds(r, rows)
             here = pl.ds(EDGE + r, rows)
-            k, zp, npart = select(tis[p + 3, block, :], [cond, z_part, n_part])
+            k, zp, npart = select(kind(p, block), [cond, z_part, n_part])
             q = qs[p + 3, here, :]
             total = qs[p + 2, here, :] + qs[p + 4, here, :]
             total = total + qs[p + 3, pl.ds(EDGE + r - 1, rows), :] + qs[p + 3, pl.ds(EDGE + r + 1, rows), :]
             total = total + jnp.where(first_lane, 0.0, pltpu.roll(q, 1, 1)) + jnp.where(last_lane, 0.0, pltpu.roll(q, ny - 1, 1))
-            ps[p + 2, here, :] = zp * vps[p + 3, block, :] + npart * total
+            ps[p + 2, here, :] = zp * field(p, block) + npart * total
             ks[p + 2, here, :] = k
 
-        @pl.when(((p < 0) & (g == 0)) | ((p >= nz) & (g == n_gz - 1)))
-        def _():
-            ks[p + 2, inside, :] = jnp.zeros((nx, ny), jnp.float32)
-
-    def z_face(p, r):
-        here = pl.ds(EDGE + r, rows)
-        k, press_here = ks[p + 2, here, :] * hinder, ps[p + 2, here, :]
-        w = k * ks[p + 3, here, :] * (press_here - ps[p + 3, here, :])
-        return k, press_here, w
-
-    def faces(p, slot, before):
+    def outside(p, ref):
+        if isinstance(p, int) and (p < 0 or p >= nz):
+            @pl.when(g == (0 if p < 0 else n_gz - 1))
+            def _():
+                ref[p + 2, inside, :] = jnp.zeros((nx, ny), jnp.float32)
+
+    def flows(p):
+        slot = lax.rem(p + 4, 2)
         for r in starts:
             block = pl.ds(r, rows)
             here = pl.ds(EDGE + r, rows)
-            k, press_here, w = z_face(p, r)
+            after = pl.ds(EDGE + r + 1, rows)
+            k_here, press_here = ks[p + 2, here, :], ps[p + 2, here, :]
+            k = k_here * hinder
+            flow[slot, 0, block, :] = k * ks[p + 3, here, :] * (press_here - ps[p + 3, here, :])
+            flow_x[slot, here, :] = k * ks[p + 2, after, :] * (press_here - ps[p + 2, after, :])
+            w_y = k * pltpu.roll(k_here, ny - 1, 1) * (press_here - pltpu.roll(press_here, ny - 1, 1))
+            flow[slot, 1, block, :] = jnp.where(last_lane, 0.0, w_y)
+
+    def first_step(p):
+        slot, source, before = lax.rem(p + 4, 4), lax.rem(p + 4, 2), lax.rem(p + 3, 4)
+        for r in starts:
+            block = pl.ds(r, rows)
+            here = pl.ds(EDGE + r, rows)
+            w = flow[source, 0, block, :]
             a = jnp.maximum(w, 0.0) + diffuse
             b = a - w
-            coef_z[slot, 0, block, :] = a
-            coef_z[slot, 1, block, :] = b
-            after = pl.ds(EDGE + r + 1, rows)
-            w_x = k * ks[p + 2, after, :] * (press_here - ps[p + 2, after, :])
-            wx[here, :] = w_x
+            w_x = flow_x[source, here, :]
             a_x = jnp.maximum(w_x, 0.0) + diffuse
             b_x = a_x - w_x
-            w_low = wx[pl.ds(EDGE + r - 1, rows), :]
+            w_low = flow_x[source, pl.ds(EDGE + r - 1, rows), :]
             a_x_low = jnp.maximum(w_low, 0.0) + diffuse
             b_x_low = a_x_low - w_low
-            k_here = ks[p + 2, here, :]
-            w_y = k * pltpu.roll(k_here, ny - 1, 1) * (press_here - pltpu.roll(press_here, ny - 1, 1))
-            w_y = jnp.where(last_lane, 0.0, w_y)
+            w_y = flow[source, 1, block, :]
             up = jnp.maximum(w_y, 0.0)
             a_y = up + diffuse
             b_y = (up - w_y) + diffuse_high
@@ -580,42 +590,38 @@
             up = jnp.maximum(w_low, 0.0)
             a_y_low = up + diffuse_low
             b_y_low = (up - w_low) + diffuse
-            (bind,) = select(tis[p + 3, block, :], [rate])
-            centre = (a + a_x) + (a_y + b_x_low) + (b_y_low + coef_z[before, 1, block, :]) + bind
-            coefs[slot, 0, block, :] = 1.0 - centre
-            coefs[slot, 1, block, :] = a_x_low
-            coefs[slot, 2, block, :] = b_x
-            coefs[slot, 3, block, :] = a_y_low
-            coefs[slot, 4, block, :] = b_y
-
-    def advance(src, p, slot, before, r):
-        block = pl.ds(r, rows)
-        here = pl.ds(EDGE + r, rows)
-        c = src[p + 2, here, :]
-        value = coefs[slot, 0, block, :] * c
-        value = value + coef_z[slot, 1, block, :] * src[p + 3, here, :] + coef_z[before, 0, block, :] * src[p + 1, here, :]
-        value = value + coefs[slot, 1, block, :] * src[p + 2, pl.ds(EDGE + r - 1, rows), :]
-        value = value + coefs[slot, 2, block, :] * src[p + 2, pl.ds(EDGE + r + 1, rows), :]
-        value = value + coefs[slot, 3, block, :] * pltpu.roll(c, 1, 1)
-        value = value + coefs[slot, 4, block, :] * pltpu.roll(c, ny - 1, 1)
-        return c, value
-
-    def first_step(p, slot, before):
-        for r in starts:
-            _, value = advance(c0, p, slot, before, r)
-            c1[p + 2, pl.ds(EDGE + r, rows), :] = value
-
-        @pl.when(((p < 0) & (g == 0)) | ((p >= nz) & (g == n_gz - 1)))
-        def _():
-            c1[p + 2, inside, :] = jnp.zeros((nx, ny), jnp.float32)
-
-    def second_step(p, slot, before):
+            (bind,) = select(kind(p, block), [rate])
+            centre = (a + a_x) + (a_y + b_x_low) + (b_y_low + coefs[before, 6, block, :]) + bind
+            centre = 1.0 - centre
+            for i, value in enumerate((centre, a_x_low, b_x, a_y_low, b_y, a, b)):
+                coefs[slot, i, block, :] = value
+            c = c0[p + 2, here, :]
+            value = centre * c + (b * c0[p + 3, here, :] + coefs[before, 5, block, :] * c0[p + 1, here, :])
+            value = value + (a_x_low * c0[p + 2, pl.ds(EDGE + r - 1, rows), :] + b_x * c0[p + 2, pl.ds(EDGE + r + 1, rows), :])
+            value = value + (a_y_low * pltpu.roll(c, 1, 1) + b_y * pltpu.roll(c, ny - 1, 1))
+            c1[p + 2, here, :] = value
+
+    def second_step(p):
+        slot, before = lax.rem(p + 4, 4), lax.rem(p + 3, 4)
         for r in starts:
             block = pl.ds(r, rows)
-            c, value = advance(c1, p, slot, before, r)
+            here = pl.ds(EDGE + r, rows)
+            c = c1[p + 2, here, :]
+            value = coefs[slot, 0, block, :] * c
+            value = value + (coefs[slot, 6, block, :] * c1[p + 3, here, :] + coefs[before, 5, block, :] * c1[p + 1, here, :])
+            value = value + (coefs[slot, 1, block, :] * c1[p + 2, pl.ds(EDGE + r - 1, rows), :]
+                             + coefs[slot, 2, block, :] * c1[p + 2, pl.ds(EDGE + r + 1, rows), :])
+            value = value + (coefs[slot, 3, block, :] * pltpu.roll(c, 1, 1) + coefs[slot, 4, block, :] * pltpu.roll(c, ny - 1, 1))
             out[p, block, :] = value
-            (bind,) = select(tis[p + 3, block, :], [rate])
-            bnd[p, block, :] = bnd[p, block, :] + bind * (c0[p + 2, pl.ds(EDGE + r, rows), :] + c)
+            (bind,) = select(kind(p, block), [rate])
+            bnd[p, block, :] = bnd[p, block, :] + bind * (c0[p + 2, here, :] + c)
+
+    def last_copies(i):
+        z0 = pl.ds(nz - chunk + i * chunk // 2, chunk // 2)
+        return [
+            pltpu.make_async_copy(out.at[z0], free_out.at[z0], out_sems.at[n_chunks - 1 + i, 0]),
+            pltpu.make_async_copy(bnd.at[z0], bound_out.at[z0], out_sems.at[n_chunks - 1 + i, 1]),
+        ]
 
     def out_copies(i):
         z0 = pl.ds(i * chunk, chunk)
@@ -624,59 +630,70 @@
             pltpu.make_async_copy(bnd.at[z0], bound_out.at[z0], out_sems.at[i, 1]),
         ]
 
-    @pl.when(has_low)
-    def _():
-        each(halo_copies(False), "wait")
-
-    each(chunk_copies(0), "wait")
-
-    for p in range(-3, 1):
-        scale(p)
-    for p in (-2, -1):
-        press(p)
-    for r in starts:
-        w = z_face(-2, r)[2]
-        a = jnp.maximum(w, 0.0) + diffuse
-        coef_z[1, 0, pl.ds(r, rows), :] = a
-        coef_z[1, 1, pl.ds(r, rows), :] = a - w
-    scale(1)
-    press(0)
-    faces(-1, 2, 1)
-    first_step(-1, 2, 1)
+    def turn(p):
+        fixed = isinstance(p, int)
+        if not fixed or 0 <= p - 4 < nz:
+            second_step(p - 4)
+        if not fixed or -1 <= p - 2 <= nz:
+            first_step(p - 2)
+            outside(p - 2, c1)
+        if not fixed or -2 <= p - 1 <= nz:
+            flows(p - 1)
+        if fixed and p == 0:
+            for r in starts:
+                block = pl.ds(r, rows)
+                w = flow[0, 0, block, :]
+                a = jnp.maximum(w, 0.0) + diffuse
+                coefs[2, 5, block, :] = a
+                coefs[2, 6, block, :] = a - w
+        if not fixed or -2 <= p + 1 <= nz + 1:
+            press(p + 1)
+            outside(p + 1, ks)
+        if not fixed or -3 <= p + 3 <= nz + 2:
+            scale(p + 3)
+
+    for p in range(-6, 4):
+        if p == 1:
+            @pl.when(has_low)
+            def _():
+                each(halo_copies(False), "wait")
+
+            each(chunk_copies(0), "wait")
+        turn(p)
 
     def body(p, _):
-        slot, before, older = lax.rem(p, 3), lax.rem(p + 2, 3), lax.rem(p + 1, 3)
-        group = lax.div(p + 2, chunk)
-
-        @pl.when((lax.rem(p + 2, chunk) == 0) & (group < n_chunks))
+        group = lax.div(p + 3, chunk)
+
+        @pl.when((lax.rem(p + 3, chunk) == 0) & (group < n_chunks))
         def _():
             each(chunk_copies(group), "wait")
 
-        @pl.when((p == nz - 2) & has_high)
+        turn(p)
+
+        @pl.when((p >= chunk + 3) & (lax.rem(p - 3, chunk) == 0))
         def _():
-            each(halo_copies(True), "wait")
-
-        scale(p + 2)
-        press(p + 1)
-        faces(p, slot, before)
-        first_step(p, slot, before)
-
-        @pl.when(p > 0)
-        def _():
-            second_step(p - 1, before, older)
-
-        @pl.when((p > 0) & (lax.rem(p, chunk) == 0))
-        def _():
-            each(out_copies(lax.div(p, chunk) - 1), "start")
+            each(out_copies(lax.div(p - 3, chunk) - 1), "start")
 
         return 0
 
-    lax.fori_loop(0, nz + 1, body, 0)
+    lax.fori_loop(4, nz - 3, body, 0)
+
+    @pl.when(has_high)
+    def _():
+        each(halo_copies(True), "wait")
+
     own = pltpu.make_async_copy(
         ps.at[pl.ds(2, nz), pl.ds(pl.multiple_of(EDGE + s * bx, 8), bx)], pressure, pressure_sem)
-    own.start()
-    for i in range(n_chunks):
+    for p in range(nz - 3, nz + 4):
+        turn(p)
+        if p == nz - 1:
+            own.start()
+            each(last_copies(0), "start")
+    each(last_copies(1), "start")
+    for i in range(n_chunks - 1):
         each(out_copies(i), "wait")
+    for i in range(2):
+        each(last_copies(i), "wait")
     own.wait()
 
 
@@ -684,6 +701,7 @@
     nz, nx, ny = conc.shape
     anywhere = pl.BlockSpec(memory_space=pl.ANY)
     scalars = pl.BlockSpec(memory_space=pltpu.SMEM)
+    vmem = pl.BlockSpec(memory_space=pltpu.VMEM)
     hbm = pl.BlockSpec(memory_space=pltpu.HBM)
     wide = nx + 2 * EDGE
     f32 = jnp.float32
@@ -696,11 +714,9 @@
             jax.ShapeDtypeStruct((nz, nx, ny), f32),
             jax.ShapeDtypeStruct((nz, nx, ny), f32),
         ),
-        in_specs=[scalars] * 5 + [pl.BlockSpec(memory_space=pltpu.VMEM), anywhere, hbm, anywhere, hbm, anywhere, hbm],
+        in_specs=[scalars] * 5 + [vmem] * 4 + [anywhere, anywhere, hbm],
         out_specs=(anywhere, anywhere, anywhere),
         scratch_shapes=[
-            pltpu.VMEM((nz + 6, nx, ny), f32),
-            pltpu.VMEM((nz + 6, nx, ny), jnp.int32),
             pltpu.VMEM((nz + 4, wide, ny), f32),
             pltpu.VMEM((nz + 4, wide, ny), f32),
             pltpu.VMEM((nz, nx, ny), f32),
@@ -708,16 +724,20 @@
             pltpu.VMEM((nz + 6, wide, ny), f32),
             pltpu.VMEM((nz + 4, wide, ny), f32),
             pltpu.VMEM((nz + 4, wide, ny), f32),
-            pltpu.VMEM((3, 2, nx, ny), f32),
-            pltpu.VMEM((wide, ny), f32),
-            pltpu.VMEM((3, 5, nx, ny), f32),
-            dma((n_chunks + 2, 4)),
-            dma((n_chunks, 2)),
+            pltpu.VMEM((2, wide, ny), f32),
+            pltpu.VMEM((2, 2, nx, ny), f32),
+            pltpu.VMEM((4, 7, nx, ny), f32),
+            dma((n_chunks + 2, 2)),
+            dma((n_chunks + 1, 2)),
             dma,
         ],
-        compiler_params=pltpu.CompilerParams(vmem_limit_bytes=60 << 20),
+        compiler_params=pltpu.CompilerParams(vmem_limit_bytes=36 << 20),
         name="transport",
-    )(cond_table, leak_table, bind_table, hindrance, diffusivity, scal, slab, tissue, thalo, conc, chalo, bound)
+    )(cond_table, leak_table, bind_table, hindrance, diffusivity, scal, slab, tissue, thalo, conc, chalo, in_hbm(bound))
+
+
+def in_hbm(array):
+    return pltpu.with_memory_space_constraint(array, pltpu.HBM)
 
 
 def solution(mesh):
@@ -725,10 +745,11 @@
 
     def local(tissue, vessel_pressure, cond_table, leak_table, bind_table, hindrance, diffusivity, free_conc, bound_conc):
         conc, bound = free_conc[0], bound_conc[0]
-        slab, thalo, chalo, scal = exchange(n_size, n_gz, cond_table, leak_table, vessel_pressure, tissue, conc)
+        slab, thalo, chalo, scal = exchange(
+            n_size, n_gz, *(in_hbm(v) for v in (cond_table, leak_table, vessel_pressure, tissue, conc)))
         pressure, free, held = transport(
-            n_gz, vessel_pressure.shape[1], cond_table, leak_table, bind_table, hindrance, diffusivity,
-            scal, slab, tissue, thalo, conc, chalo, bound)
+            n_gz, vessel_pressure.shape[1], *(in_hbm(v) for v in (cond_table, leak_table, bind_table)), hindrance, diffusivity,
+            scal, slab, tissue, thalo, conc, chalo, in_hbm(bound))
         return pressure, free[None], held[None]
 
     return jax.shard_map(

time: 60.1 us -> 51.9 us (0.86)
  the two profiles are of different devices: /device:TPU:1 before, /device:TPU:6 now
where the time goes in v3:
time: 51.9 us; the launch traced here: 51 us
  Pallas kernels  49 us (94%)
  between operations  1.96 us (4%)
    pallas_call x1, Pallas kernels, exchange(): pl.pallas_call(functools.partial(exchange_kernel, n_size, n_gz), out_shap...  36.2 us
    pallas_call x1, Pallas kernels, transport(): pl.pallas_call(functools.partial(transport_kernel, n_gz), out_shape=(jax....  12.8 us

profile of v3, /device:TPU:6, one launch (start us, length us, event | category | flops | bytes accessed | tf_op | source)
XLA Modules:
  0.0 51.0 jit_solution(11414278423756422151)
XLA Ops:
  1.9 0.0 copy-start
  1.9 0.0 copy-start.1
  1.9 36.2 %exchange.1 = (f32[38,128,128]{2,1,0:T(8,128)S(1)}, s32[6,128,128]{2,1,0:T(8,128)S(1)}, f32[4,128,128]{2,1,0:T(8,128)S(1)}, f32[8,128]{1,0:T(8,128)S(1)}) custom-call(f32[3]{0:T(128)} %cond_ref.3, f32[3]{0:T(128)} %leak_ref.3, f32[32,16,128]{2,1,0:T(8,128)} %vp.1, s32[32,128,128]{2,1,0:T(8,128)} %tissue.3, f32[32,128,128]{2,1,0:T(8,128)} %bitcast.4), custom_call_target="tpu_custom_call" | custom-call | tf_op jit(solution)/shard_map/exchange/pallas_call | solution.py:409
  38.2 0.0 copy-done
  38.2 0.0 copy-done.1
  38.2 12.8 %transport.1 = (f32[32,16,128]{2,1,0:T(8,128)}, f32[32,128,128]{2,1,0:T(8,128)}, f32[32,128,128]{2,1,0:T(8,128)}) custom-call(f32[3]{0:T(128)} %cond_ref.3, f32[3]{0:T(128)} %leak_ref.3, f32[1,3]{1,0:T(1,128)} %bind_ref.1, f32[1]{0:T(128)S(6)} %copy.12.hinder_ref, f32[1]{0:T(128)S(6)} %copy.13.diffuse_ref, f32[8,128]{1,0:T(8,128)S(1)} %get-tuple-element.10.scal, ...), custom_call_target="tpu_custom_call" | custom-call | tf_op jit(solution)/shard_map/transport/pallas_call | solution.py:710
Async XLA Ops:
  1.9 36.3 %copy-start = (s32[32,128,128]{2,1,0:T(8,128)S(1)}, s32[32,128,128]{2,1,0:T(8,128)}, u32[]{:S(2)}) copy-start(s32[32,128,128]{2,1,0:T(8,128)} %tissue.3) | copy-start | bytes 6291460
  1.9 36.3 %copy-start.1 = (f32[1,32,128,128]{3,2,1,0:T(8,128)S(1)}, f32[1,32,128,128]{3,2,1,0:T(8,128)}, u32[]{:S(2)}) copy-start(f32[1,32,128,128]{3,2,1,0:T(8,128)} %param.16) | copy-start | bytes 6291460

commit v4 on v3

--- a/solution.py
+++ b/solution.py
@@ -279,8 +279,6 @@
         return 0
 
     lax.fori_loop(0, nz + 4, scale, 0, unroll=4)
-    hand_on(order[0])
-
     def stencil(ref, e):
         q = ref[e]
         total = ref[e - 1] + ref[e + 1] + pltpu.roll(q, 1, 0) + pltpu.roll(q, wide - 1, 0)
@@ -314,8 +312,7 @@
     apply(nz + 2)
     zero = jnp.zeros((bx, ny), jnp.float32)
     sums = lax.fori_loop(2, nz + 2, first_sums, ((zero, zero),) * 3, unroll=2)
-    hand_on(order[1])
-    hand_far(order[0])
+    hand_on(order[0])
 
     def last_sum(e, acc):
         labels = tex[e]
@@ -358,12 +355,19 @@
         return add_tiles([slots[i] for i in range(count)])
 
     def first_half():
+        hand_on(order[1])
+        hand_far(order[0])
         hand_on(order[2])
         hand_far(order[1])
+        hand_on(order[3])
 
     def second_half():
-        hand_on(order[3])
         hand_far(order[2])
+        hand_far(order[3])
+        own.wait()
+        for c in order[:2]:
+            finish(c)
+        start_all(edges)
 
     total_tile[...] = reduce(tile, red_size, s, n_size, "size", ring_send, ring_recv, first_half)
     total = reduce(total_tile, red_gz, g, n_gz, "gz", grid_send, grid_recv, second_half)
@@ -385,11 +389,6 @@
     y_part = -(b0 * v) / det
     scal[...] = jnp.where(row == 0, x_part + y_part * (1.0 - t), -y_part)
 
-    own.wait()
-    for c in order[:2]:
-        finish(c)
-    start_all(edges)
-    hand_far(order[3])
     for c in order[2:]:
         finish(c)
     for c in order:

time: 51.9 us -> 49 us (0.944); the launches traced: 51 us -> 48.9 us
  Pallas kernels: 49 us -> 46.9 us
    pallas_call x1, Pallas kernels: 36.2 us -> 34.1 us  [exchange(): pl.pallas_call(functools.partial(exchange_kernel, n_size, n_gz), out_shap...]
where the time goes in v4:
time: 49 us; the launch traced here: 48.9 us
  Pallas kernels  46.9 us (96%)
  between operations  1.96 us (4%)
    pallas_call x1, Pallas kernels, exchange(): pl.pallas_call(functools.partial(exchange_kernel, n_size, n_gz), out_shap...  34.1 us
    pallas_call x1, Pallas kernels, transport(): pl.pallas_call(functools.partial(transport_kernel, n_gz), out_shape=(jax....  12.8 us

profile of v4, /device:TPU:6, one launch (start us, length us, event | category | flops | bytes accessed | tf_op | source)
XLA Modules:
  0.0 48.9 jit_solution(4161841860606407231)
XLA Ops:
  1.9 0.0 copy-start
  1.9 0.0 copy-start.1
  1.9 34.1 %exchange.1 = (f32[38,128,128]{2,1,0:T(8,128)S(1)}, s32[6,128,128]{2,1,0:T(8,128)S(1)}, f32[4,128,128]{2,1,0:T(8,128)S(1)}, f32[8,128]{1,0:T(8,128)S(1)}) custom-call(f32[3]{0:T(128)} %cond_ref.3, f32[3]{0:T(128)} %leak_ref.3, f32[32,16,128]{2,1,0:T(8,128)} %vp.1, s32[32,128,128]{2,1,0:T(8,128)} %tissue.3, f32[32,128,128]{2,1,0:T(8,128)} %bitcast.4), custom_call_target="tpu_custom_call" | custom-call | tf_op jit(solution)/shard_map/exchange/pallas_call | solution.py:408
  36.0 0.0 copy-done
  36.0 0.0 copy-done.1
  36.0 12.8 %transport.1 = (f32[32,16,128]{2,1,0:T(8,128)}, f32[32,128,128]{2,1,0:T(8,128)}, f32[32,128,128]{2,1,0:T(8,128)}) custom-call(f32[3]{0:T(128)} %cond_ref.3, f32[3]{0:T(128)} %leak_ref.3, f32[1,3]{1,0:T(1,128)} %bind_ref.1, f32[1]{0:T(128)S(6)} %copy.12.hinder_ref, f32[1]{0:T(128)S(6)} %copy.13.diffuse_ref, f32[8,128]{1,0:T(8,128)S(1)} %get-tuple-element.10.scal, ...), custom_call_target="tpu_custom_call" | custom-call | tf_op jit(solution)/shard_map/transport/pallas_call | solution.py:709
Async XLA Ops:
  1.9 34.1 %copy-start = (s32[32,128,128]{2,1,0:T(8,128)S(1)}, s32[32,128,128]{2,1,0:T(8,128)}, u32[]{:S(2)}) copy-start(s32[32,128,128]{2,1,0:T(8,128)} %tissue.3) | copy-start | bytes 6291460
  1.9 34.1 %copy-start.1 = (f32[1,32,128,128]{3,2,1,0:T(8,128)S(1)}, f32[1,32,128,128]{3,2,1,0:T(8,128)}, u32[]{:S(2)}) copy-start(f32[1,32,128,128]{3,2,1,0:T(8,128)} %param.16) | copy-start | bytes 6291460

commit v5 on v4

--- a/solution.py
+++ b/solution.py
@@ -440,7 +440,7 @@
 def transport_kernel(
     n_gz, cond_ref, leak_ref, bind_ref, hinder_ref, diffuse_ref, scal, slab, tissue, thalo, conc, chalo, bound,
     pressure, free_out, bound_out,
-    c0, c1, bnd, out, qs, ps, ks, flow_x, flow, coefs, sems, out_sems, pressure_sem,
+    c0, c1, bnd, out, qs, ps, ks, flow_x, flow, coefs, coef_z, sems, out_sems, pressure_sem,
 ):
     s, g = lax.axis_index("size"), lax.axis_index("gz")
     nz, nx, ny = conc.shape
@@ -572,6 +572,8 @@
         for r in starts:
             block = pl.ds(r, rows)
             here = pl.ds(EDGE + r, rows)
+            a_low, b_low = coef_z[before, 0, block, :], coef_z[before, 1, block, :]
+            c, c_above, c_below = c0[p + 2, here, :], c0[p + 3, here, :], c0[p + 1, here, :]
             w = flow[source, 0, block, :]
             a = jnp.maximum(w, 0.0) + diffuse
             b = a - w
@@ -590,15 +592,16 @@
             a_y_low = up + diffuse_low
             b_y_low = (up - w_low) + diffuse
             (bind,) = select(kind(p, block), [rate])
-            centre = (a + a_x) + (a_y + b_x_low) + (b_y_low + coefs[before, 6, block, :]) + bind
+            centre = (a + a_x) + (a_y + b_x_low) + (b_y_low + b_low) + bind
             centre = 1.0 - centre
-            for i, value in enumerate((centre, a_x_low, b_x, a_y_low, b_y, a, b)):
-                coefs[slot, i, block, :] = value
-            c = c0[p + 2, here, :]
-            value = centre * c + (b * c0[p + 3, here, :] + coefs[before, 5, block, :] * c0[p + 1, here, :])
+            value = centre * c + (b * c_above + a_low * c_below)
             value = value + (a_x_low * c0[p + 2, pl.ds(EDGE + r - 1, rows), :] + b_x * c0[p + 2, pl.ds(EDGE + r + 1, rows), :])
             value = value + (a_y_low * pltpu.roll(c, 1, 1) + b_y * pltpu.roll(c, ny - 1, 1))
             c1[p + 2, here, :] = value
+            for i, value in enumerate((centre, a_x_low, b_x, a_y_low, b_y)):
+                coefs[slot, i, block, :] = value
+            coef_z[slot, 0, block, :] = a
+            coef_z[slot, 1, block, :] = b
 
     def second_step(p):
         slot, before = lax.rem(p + 4, 4), lax.rem(p + 3, 4)
@@ -606,14 +609,15 @@
             block = pl.ds(r, rows)
             here = pl.ds(EDGE + r, rows)
             c = c1[p + 2, here, :]
+            held, earlier = bnd[p, block, :], c0[p + 2, here, :]
             value = coefs[slot, 0, block, :] * c
-            value = value + (coefs[slot, 6, block, :] * c1[p + 3, here, :] + coefs[before, 5, block, :] * c1[p + 1, here, :])
+            value = value + (coef_z[slot, 1, block, :] * c1[p + 3, here, :] + coef_z[before, 0, block, :] * c1[p + 1, here, :])
             value = value + (coefs[slot, 1, block, :] * c1[p + 2, pl.ds(EDGE + r - 1, rows), :]
                              + coefs[slot, 2, block, :] * c1[p + 2, pl.ds(EDGE + r + 1, rows), :])
             value = value + (coefs[slot, 3, block, :] * pltpu.roll(c, 1, 1) + coefs[slot, 4, block, :] * pltpu.roll(c, ny - 1, 1))
             out[p, block, :] = value
             (bind,) = select(kind(p, block), [rate])
-            bnd[p, block, :] = bnd[p, block, :] + bind * (c0[p + 2, here, :] + c)
+            bnd[p, block, :] = held + bind * (earlier + c)
 
     def last_copies(i):
         z0 = pl.ds(nz - chunk + i * chunk // 2, chunk // 2)
@@ -643,8 +647,8 @@
                 block = pl.ds(r, rows)
                 w = flow[0, 0, block, :]
                 a = jnp.maximum(w, 0.0) + diffuse
-                coefs[2, 5, block, :] = a
-                coefs[2, 6, block, :] = a - w
+                coef_z[2, 0, block, :] = a
+                coef_z[2, 1, block, :] = a - w
         if not fixed or -2 <= p + 1 <= nz + 1:
             press(p + 1)
             outside(p + 1, ks)
@@ -725,7 +729,8 @@
             pltpu.VMEM((nz + 4, wide, ny), f32),
             pltpu.VMEM((2, wide, ny), f32),
             pltpu.VMEM((2, 2, nx, ny), f32),
-            pltpu.VMEM((4, 7, nx, ny), f32),
+            pltpu.VMEM((4, 5, nx, ny), f32),
+            pltpu.VMEM((4, 2, nx, ny), f32),
             dma((n_chunks + 2, 2)),
             dma((n_chunks + 1, 2)),
             dma,

time: 49 us -> 48.4 us (0.988)
  Pallas kernels: 46.9 us -> 46.3 us
    pallas_call x1, Pallas kernels: 12.8 us -> 12.2 us  [transport(): pl.pallas_call(functools.partial(transport_kernel, n_gz), out_shape=(jax....]
where the time goes in v5:
time: 48.4 us; the launch traced here: 48.2 us
  Pallas kernels  46.3 us (96%)
  between operations  1.96 us (4%)
    pallas_call x1, Pallas kernels, exchange(): pl.pallas_call(functools.partial(exchange_kernel, n_size, n_gz), out_shap...  34.1 us
    pallas_call x1, Pallas kernels, transport(): pl.pallas_call(functools.partial(transport_kernel, n_gz), out_shape=(jax....  12.2 us

profile of v5, /device:TPU:6, one launch (start us, length us, event | category | flops | bytes accessed | tf_op | source)
XLA Modules:
  0.0 48.2 jit_solution(14896896694584735247)
XLA Ops:
  1.9 0.0 copy-start
  1.9 0.0 copy-start.1
  1.9 34.1 %exchange.1 = (f32[38,128,128]{2,1,0:T(8,128)S(1)}, s32[6,128,128]{2,1,0:T(8,128)S(1)}, f32[4,128,128]{2,1,0:T(8,128)S(1)}, f32[8,128]{1,0:T(8,128)S(1)}) custom-call(f32[3]{0:T(128)} %cond_ref.3, f32[3]{0:T(128)} %leak_ref.3, f32[32,16,128]{2,1,0:T(8,128)} %vp.1, s32[32,128,128]{2,1,0:T(8,128)} %tissue.3, f32[32,128,128]{2,1,0:T(8,128)} %bitcast.4), custom_call_target="tpu_custom_call" | custom-call | tf_op jit(solution)/shard_map/exchange/pallas_call | solution.py:408
  36.0 0.0 copy-done
  36.0 0.0 copy-done.1
  36.0 12.2 %transport.1 = (f32[32,16,128]{2,1,0:T(8,128)}, f32[32,128,128]{2,1,0:T(8,128)}, f32[32,128,128]{2,1,0:T(8,128)}) custom-call(f32[3]{0:T(128)} %cond_ref.3, f32[3]{0:T(128)} %leak_ref.3, f32[1,3]{1,0:T(1,128)} %bind_ref.1, f32[1]{0:T(128)S(6)} %copy.12.hinder_ref, f32[1]{0:T(128)S(6)} %copy.13.diffuse_ref, f32[8,128]{1,0:T(8,128)S(1)} %get-tuple-element.10.scal, ...), custom_call_target="tpu_custom_call" | custom-call | tf_op jit(solution)/shard_map/transport/pallas_call | solution.py:713
Async XLA Ops:
  1.9 34.1 %copy-start = (s32[32,128,128]{2,1,0:T(8,128)S(1)}, s32[32,128,128]{2,1,0:T(8,128)}, u32[]{:S(2)}) copy-start(s32[32,128,128]{2,1,0:T(8,128)} %tissue.3) | copy-start | bytes 6291460
  1.9 34.1 %copy-start.1 = (f32[1,32,128,128]{3,2,1,0:T(8,128)S(1)}, f32[1,32,128,128]{3,2,1,0:T(8,128)}, u32[]{:S(2)}) copy-start(f32[1,32,128,128]{3,2,1,0:T(8,128)} %param.16) | copy-start | bytes 6291460

commit v6 on v5

--- a/solution.py
+++ b/solution.py
@@ -620,7 +620,8 @@
             bnd[p, block, :] = held + bind * (earlier + c)
 
     def last_copies(i):
-        z0 = pl.ds(nz - chunk + i * chunk // 2, chunk // 2)
+        first, count = ((nz - 8, 4), (nz - 4, 2), (nz - 2, 2))[i]
+        z0 = pl.ds(first, count)
         return [
             pltpu.make_async_copy(out.at[z0], free_out.at[z0], out_sems.at[n_chunks - 1 + i, 0]),
             pltpu.make_async_copy(bnd.at[z0], bound_out.at[z0], out_sems.at[n_chunks - 1 + i, 1]),
@@ -692,10 +693,12 @@
         if p == nz - 1:
             own.start()
             each(last_copies(0), "start")
-    each(last_copies(1), "start")
+        if p == nz + 1:
+            each(last_copies(1), "start")
+    each(last_copies(2), "start")
     for i in range(n_chunks - 1):
         each(out_copies(i), "wait")
-    for i in range(2):
+    for i in range(3):
         each(last_copies(i), "wait")
     own.wait()
 
@@ -732,7 +735,7 @@
             pltpu.VMEM((4, 5, nx, ny), f32),
             pltpu.VMEM((4, 2, nx, ny), f32),
             dma((n_chunks + 2, 2)),
-            dma((n_chunks + 1, 2)),
+            dma((n_chunks + 2, 2)),
             dma,
         ],
         compiler_params=pltpu.CompilerParams(vmem_limit_bytes=36 << 20),

time: 48.4 us -> 48.4 us (level)
  no operation moved by 1% of the time
where the time goes in v6:
time: 48.4 us; the launch traced here: 48.2 us
  Pallas kernels  46.2 us (95%)
  between operations  1.96 us (4%)
    pallas_call x1, Pallas kernels, exchange(): pl.pallas_call(functools.partial(exchange_kernel, n_size, n_gz), out_shap...  34.1 us
    pallas_call x1, Pallas kernels, transport(): pl.pallas_call(functools.partial(transport_kernel, n_gz), out_shape=(jax....  12.2 us

profile of v6, /device:TPU:6, one launch (start us, length us, event | category | flops | bytes accessed | tf_op | source)
XLA Modules:
  0.0 48.2 jit_solution(16253823147052800071)
XLA Ops:
  1.9 0.0 copy-start
  1.9 0.0 copy-start.1
  1.9 34.1 %exchange.1 = (f32[38,128,128]{2,1,0:T(8,128)S(1)}, s32[6,128,128]{2,1,0:T(8,128)S(1)}, f32[4,128,128]{2,1,0:T(8,128)S(1)}, f32[8,128]{1,0:T(8,128)S(1)}) custom-call(f32[3]{0:T(128)} %cond_ref.3, f32[3]{0:T(128)} %leak_ref.3, f32[32,16,128]{2,1,0:T(8,128)} %vp.1, s32[32,128,128]{2,1,0:T(8,128)} %tissue.3, f32[32,128,128]{2,1,0:T(8,128)} %bitcast.4), custom_call_target="tpu_custom_call" | custom-call | tf_op jit(solution)/shard_map/exchange/pallas_call | solution.py:408
  36.0 0.0 copy-done
  36.0 0.0 copy-done.1
  36.0 12.2 %transport.1 = (f32[32,16,128]{2,1,0:T(8,128)}, f32[32,128,128]{2,1,0:T(8,128)}, f32[32,128,128]{2,1,0:T(8,128)}) custom-call(f32[3]{0:T(128)} %cond_ref.3, f32[3]{0:T(128)} %leak_ref.3, f32[1,3]{1,0:T(1,128)} %bind_ref.1, f32[1]{0:T(128)S(6)} %copy.12.hinder_ref, f32[1]{0:T(128)S(6)} %copy.13.diffuse_ref, f32[8,128]{1,0:T(8,128)S(1)} %get-tuple-element.10.scal, ...), custom_call_target="tpu_custom_call" | custom-call | tf_op jit(solution)/shard_map/transport/pallas_call | solution.py:716
Async XLA Ops:
  1.9 34.1 %copy-start = (s32[32,128,128]{2,1,0:T(8,128)S(1)}, s32[32,128,128]{2,1,0:T(8,128)}, u32[]{:S(2)}) copy-start(s32[32,128,128]{2,1,0:T(8,128)} %tissue.3) | copy-start | bytes 6291460
  1.9 34.1 %copy-start.1 = (f32[1,32,128,128]{3,2,1,0:T(8,128)S(1)}, f32[1,32,128,128]{3,2,1,0:T(8,128)}, u32[]{:S(2)}) copy-start(f32[1,32,128,128]{3,2,1,0:T(8,128)} %param.16) | copy-start | bytes 6291460
